TPU v7x, 256 devices: a whole 4x4x8 slice. The times are simulated.
256 devices in a mesh: req: 32 (over z, x), head: 8 (over y, core).
Axes of the slice: x: 4, y: 4, z: 8, core: 2. Of those that a mesh axis runs over, the one named last changes fastest.
Arguments:
- hidden: bfloat16 [64, 128, 8192], P('req', None, 'head'), may hold values from -6 to 6
- w_query: bfloat16 [8192, 8192], P('req', 'head'), may hold values from -0.0625 to 0.0625
- w_key: bfloat16 [8192, 1024], P('req', 'head'), may hold values from -0.0625 to 0.0625
- w_value: bfloat16 [8192, 1024], P('req', 'head'), may hold values from -0.0625 to 0.0625
- doc_keys: bfloat16 [512, 8, 128, 128], P('req', 'head'), may hold values from -320 to 320
- doc_values: bfloat16 [512, 8, 128, 128], P('req', 'head'), may hold values from -8 to 8
- slot_counts: int32 [512, 8], P(None, 'head'), may hold values from 1 to 8
- kept_blocks: int32 [512, 8, 8], P(None, 'head'), may hold values from 0 to 15, as said below
- doc_ids: int32 [64, 16], replicated, may hold values from 0 to 511, as said below
- doc_place: int32 [512], replicated, may hold values from 0 to 511, as said below
- recompute_rows: int32 [64, 128], P('req'), may hold values from 0 to 4095, as said below
Outputs:
- attended: bfloat16 [64, 128, 8192], P('req', None, 'head')
- new_keys: bfloat16 [64, 128, 1024], P('req', None, 'head')
- new_values: bfloat16 [64, 128, 1024], P('req', None, 'head')
Inputs may be any that keep to these rules, and one draw needn't show every extreme that they name: `doc_ids`: among the 32 document slots of the requests of one index of req, at most 2 name documents whose doc_place lies in one owner's 16 rows, counting repeats; in every such block some owner has exactly 2. `doc_place`: a permutation; document d sits on owner doc_place[d] // 16. `kept_blocks`: for each document and head the 8 entries are distinct and rising. `recompute_rows`: distinct and rising within a request.
All inputs are finite; a program needn't handle non-finite values.
Results may differ from a plain program's by a relative error of at most 0.0085.
The roundings to bfloat16 on the way count: a program that leaves them out, or rounds other values in their place, can miss the bound.
Values may be sent and summed in bfloat16 or wider, within the bound.
A program may use at most 128 MiB of HBM per device.

v0:
```python
import math

import jax
import jax.numpy as jnp
from jax import lax
from jax.sharding import PartitionSpec as P

QH = 64
KVH = 8
HD = 128
BLK = 16
DOC_BLKS = 16
SLOTS = 8
NDOC = 16


def attend(block_queries, context_keys, context_values, live, scale):
    scores = (
        jnp.einsum("rgd,kd->rgk", block_queries, context_keys, preferred_element_type=jnp.float32)
        * scale
    )
    scores = jnp.where(live[None, None, :], scores, -jnp.inf)
    peak = jnp.max(scores, axis=-1, keepdims=True)
    weights = jnp.exp(scores - peak)
    probs = (weights / jnp.sum(weights, axis=-1, keepdims=True)).astype(jnp.bfloat16)
    result = jnp.einsum("rgk,kd->rgd", probs, context_values, preferred_element_type=jnp.float32)
    return result.astype(jnp.bfloat16).reshape(block_queries.shape[0], -1)


def shards(
    hidden,
    w_query,
    w_key,
    w_value,
    doc_keys,
    doc_values,
    slot_counts,
    kept_blocks,
    doc_ids,
    doc_place,
    recompute_rows,
):
    req_here, rows_req, width_part = hidden.shape
    total = req_here * rows_req
    heads_here = w_key.shape[1] // HD
    group = QH // KVH
    span = SLOTS * BLK
    scale = 1.0 / math.sqrt(HD)
    owners = lax.axis_size("req")
    mine = lax.axis_index("req")
    docs_here = doc_keys.shape[0]
    refs = req_here * NDOC
    capacity = 2 * (refs // owners)
    whole = lax.all_gather(hidden, "head", axis=2, tiled=True).reshape(total, -1)
    pieces = (
        lax.all_gather(w_query, "req", axis=0, tiled=True),
        lax.all_gather(w_key, "req", axis=0, tiled=True),
        lax.all_gather(w_value, "req", axis=0, tiled=True),
    )
    sums = tuple((jnp.dot(whole, piece, preferred_element_type=jnp.float32) for piece in pieces))
    placed = doc_place[doc_ids]
    owner_all = (placed // docs_here).reshape(owners, refs)
    local_all = (placed % docs_here).reshape(owners, refs)
    order = jnp.arange(refs, dtype=jnp.int32)
    earlier = (owner_all[:, :, None] == owner_all[:, None, :]) & (
        order[None, None, :] < order[None, :, None]
    )
    rank = jnp.sum(earlier.astype(jnp.int32), axis=2)
    slot_ids = jnp.arange(capacity, dtype=jnp.int32)
    match = (
        (owner_all == mine)[:, :, None] & (rank[:, :, None] == slot_ids[None, None, :])
    ).astype(jnp.int32)
    picked = jnp.sum(match * local_all[:, :, None], axis=1)
    used = jnp.sum(match, axis=1) > 0

    def pack(cache):
        selected = cache[picked]
        return jnp.where(used[:, :, None, None, None], selected, jnp.zeros_like(selected))

    got_keys = lax.all_to_all(pack(doc_keys), "req", split_axis=0, concat_axis=0, tiled=True)
    got_values = lax.all_to_all(pack(doc_values), "req", split_axis=0, concat_axis=0, tiled=True)
    own_owner = lax.dynamic_index_in_dim(owner_all, mine, 0, False)
    own_rank = lax.dynamic_index_in_dim(rank, mine, 0, False)
    where_row = own_owner * capacity + own_rank
    tail = got_keys.shape[2:]
    fetched_keys = got_keys.reshape((owners * capacity,) + tail)[where_row].reshape(
        (req_here, NDOC) + tail
    )
    fetched_values = got_values.reshape((owners * capacity,) + tail)[where_row].reshape(
        (req_here, NDOC) + tail
    )
    fetched_keys, fetched_values = (fetched_keys, fetched_values)
    queries = sums[0].astype(jnp.bfloat16).reshape(req_here, rows_req, heads_here, group, HD)
    keys_new = sums[1].astype(jnp.bfloat16).reshape(req_here, rows_req, heads_here, HD)
    values_new = sums[2].astype(jnp.bfloat16).reshape(req_here, rows_req, heads_here, HD)
    my_ids = lax.dynamic_slice_in_dim(doc_ids, mine * req_here, req_here, 0)
    offsets = jnp.arange(NDOC, dtype=jnp.int32)[:, None, None] * (DOC_BLKS * BLK)
    inner = jnp.arange(BLK, dtype=jnp.int32)[None, None, :]
    slot_index = jnp.arange(SLOTS, dtype=jnp.int32)[None, :, None]
    block_rows = 128
    request_outputs = []
    for request in range(req_here):
        ids = my_ids[request]
        positions = recompute_rows[request]
        blocks = kept_blocks[ids, 0]
        count_here = slot_counts[ids, 0]
        key_pos = (offsets + blocks[:, :, None] * BLK + inner).reshape(-1)
        valid = (slot_index < count_here[:, None, None]) & (inner >= 0)
        replaced = jnp.any(key_pos[:, None] == positions[None, :], axis=1)
        live = jnp.concatenate(
            [valid.reshape(-1) & jnp.logical_not(replaced), jnp.ones((rows_req,), bool)]
        )
        context_keys = jnp.concatenate(
            [fetched_keys[request, :, 0].reshape(NDOC * span, HD), keys_new[request, :, 0]], axis=0
        )
        context_values = jnp.concatenate(
            [fetched_values[request, :, 0].reshape(NDOC * span, HD), values_new[request, :, 0]],
            axis=0,
        )
        query_blocks = queries[request, :, 0].reshape(rows_req // block_rows, block_rows, group, HD)
        result = lax.map(
            lambda block_queries: attend(block_queries, context_keys, context_values, live, scale),
            query_blocks,
        )
        head_outputs = result.reshape(rows_req, group * HD)
        request_outputs.append(head_outputs)
    attended = jnp.stack(request_outputs, axis=0)
    return (
        attended,
        keys_new.reshape(req_here, rows_req, heads_here * HD),
        values_new.reshape(req_here, rows_req, heads_here * HD),
    )


def solution(mesh):
    return jax.shard_map(
        shards,
        mesh=mesh,
        in_specs=(
            P("req", None, "head"),
            P("req", "head"),
            P("req", "head"),
            P("req", "head"),
            P("req", "head", None, None),
            P("req", "head", None, None),
            P(None, "head"),
            P(None, "head", None),
            P(),
            P(),
            P("req", None),
        ),
        out_specs=(P("req", None, "head"), P("req", None, "head"), P("req", None, "head")),
        check_vma=False,
    )
```

profile of v0, /device:TPU:1, one launch (start us, length us, event | category | flops | bytes accessed | tf_op | source)
XLA Modules:
  0.0 391.2 jit_solution(2482674667444475200)
XLA Ops:
  10.9 6.9 %gather_fusion.2 = s32[1024]{0:T(1024)S(1)} fusion(s32[512]{0:T(512)S(1)} %copy-done.1, s32[1024]{0:T(1024)S(1)} %broadcast_clamp_fusion), kind=kCustom, calls=%fused_computation.2 | custom fusion | bytes 12288 | tf_op jit(solution)/shard_map/gather | solution.py:61
  17.9 0.8 convert_reduce_fusion
  19.2 1.0 gather_fusion.5
  20.1 2.1 gather_fusion.3
  22.2 3.3 broadcast_select_fusion
  25.6 68.4 %all_to_all.10 = bf16[32,2,1,128,128]{4,3,1,2,0:T(8,128)(2,1)} all-to-all(bf16[32,2,1,128,128]{4,3,1,2,0:T(8,128)(2,1)S(1)} %get-tuple-element.55), channel_id=1, replica_groups=mesh['req'=32,'head'=8] {'req'}, dimensions={0} | all-to-all | bytes 4194304 | tf_op jit(solution)/shard_map/all_to_all | solution.py:81
  94.0 7.5 %all-to-all-start = ((bf16[32,2,1,128,128]{4,3,1,2,0:T(8,128)(2,1)}), bf16[32,2,1,128,128]{4,3,1,2,0:T(8,128)(2,1)S(1)}, u32[]{:S(2)}, u32[]{:S(2)}) async-start(bf16[32,2,1,128,128]{4,3,1,2,0:T(8,128)(2,1)} %get-tuple-element.56), calls=%async_computation | async-start | bytes 4194304 | tf_op jit(solution)/shard_map/all_to_all | solution.py:80
  106.6 3.3 gather_fusion.6
  110.0 2.1 fusion.80
  112.0 2.1 copy.60
  114.1 1.0 copy.61
  115.1 34.6 %all-to-all-done = bf16[32,2,1,128,128]{4,3,1,2,0:T(8,128)(2,1)S(1)} async-done(((bf16[32,2,1,128,128]{4,3,1,2,0:T(8,128)(2,1)}), bf16[32,2,1,128,128]{4,3,1,2,0:T(8,128)(2,1)S(1)}, u32[]{:S(2)}, u32[]{:S(2)}) %all-to-all-start) | async-done | bytes 2097184 | tf_op jit(solution)/shard_map/all_to_all | solution.py:80
  149.8 1.7 gather_fusion.4
  151.5 1.3 fusion.81
  152.9 4.1 %convolution_convert_fusion.1 = bf16[256,128]{1,0:T(8,128)(2,1)S(1)} fusion(bf16[256,8192]{1,0:T(8,128)(2,1)} %bitcast.102, bf16[8192,128]{1,0:T(8,128)(2,1)} %all-gather.11.cloned.1.call-done), kind=kOutput, calls=%fused_computation.34 | convolution fusion | flops 536903680 | bytes 6356992 | tf_op jit(solution)/shard_map/dot_general | solution.py:60
  157.3 56.9 %all-gather.9.cloned.1.call-done = bf16[8192,128]{1,0:T(8,128)(2,1)} async-done(((bf16[256,128]{1,0:T(8,128)(2,1)}), bf16[8192,128]{1,0:T(8,128)(2,1)}) %all-gather.9.cloned.1.call-update) | async-done | bytes 2097168 | tf_op jit(solution)/shard_map/all_gather | solution.py:57
  214.1 4.1 %convolution_convert_fusion.2 = bf16[256,128]{1,0:T(8,128)(2,1)S(1)} fusion(bf16[256,8192]{1,0:T(8,128)(2,1)} %bitcast.103, bf16[8192,128]{1,0:T(8,128)(2,1)} %all-gather.9.cloned.1.call-done), kind=kOutput, calls=%fused_computation.35 | convolution fusion | flops 536903680 | bytes 6356992 | tf_op jit(solution)/shard_map/dot_general | solution.py:60
  218.3 139.6 %all-gather.7.cloned.1.call-done = bf16[8192,1024]{1,0:T(8,128)(2,1)} async-done(((bf16[256,1024]{1,0:T(8,128)(2,1)}), bf16[8192,1024]{1,0:T(8,128)(2,1)}) %all-gather.7.cloned.1.call-update) | async-done | bytes 16777232 | tf_op jit(solution)/shard_map/all_gather | solution.py:56
  357.9 11.5 %convolution_convert_fusion = bf16[256,1024]{1,0:T(8,128)(2,1)S(1)} fusion(bf16[256,8192]{1,0:T(8,128)(2,1)} %bitcast.104, bf16[8192,1024]{1,0:T(8,128)(2,1)} %all-gather.7.cloned.1.call-done), kind=kOutput, calls=%fused_computation.31 | convolution fusion | flops 4295229440 | bytes 21495808 | tf_op jit(solution)/shard_map/dot_general | solution.py:60
  369.5 3.6 fusion.84
  373.1 3.5 fusion.16
  376.8 3.4 fusion.87
  380.1 3.5 fusion.17
  383.8 0.8 pad_maximum_fusion
  (81 shorter events, 9.9 us)
Async XLA Ops:
  7.2 12.0 %copy-start = (bf16[16,1,128,128]{3,2,1,0:T(8,128)(2,1)S(1)}, bf16[16,1,128,128]{3,2,1,0:T(8,128)(2,1)}, u32[]{:S(2)}) copy-start(bf16[16,1,128,128]{3,2,1,0:T(8,128)(2,1)} %param.16) | copy-start | bytes 1572868
  7.2 3.7 copy-start.1
  7.2 145.6 %all-gather.11.cloned.1.call-start = ((), (), s32[]{:S(2)}) async-start(), calls=%async_computation.5 | async-start | bytes 2162688 | tf_op jit(solution)/shard_map/all_gather | solution.py:58
  7.9 144.9 %all-gather.5.cloned.1.call-start = ((), (), s32[]{:S(2)}) async-start(), calls=%async_computation.2 | async-start | bytes 4718592 | tf_op jit(solution)/shard_map/all_gather | solution.py:54
  8.7 205.4 %all-gather.9.cloned.1.call-start = ((), (), s32[]{:S(2)}) async-start(), calls=%async_computation.4 | async-start | bytes 2162688 | tf_op jit(solution)/shard_map/all_gather | solution.py:57
  9.4 348.5 %all-gather.7.cloned.1.call-start = ((), (), s32[]{:S(2)}) async-start(), calls=%async_computation.3 | async-start | bytes 17301504 | tf_op jit(solution)/shard_map/all_gather | solution.py:56
  17.7 2.4 copy-start.3
  25.6 75.9 %copy-start.8 = (s32[64,16]{0,1:T(8,128)S(1)}, s32[64,16]{0,1:T(8,128)}, u32[]{:S(2)}) copy-start(s32[64,16]{0,1:T(8,128)} %param.19) | copy-start | bytes 12292
  25.6 76.1 %copy-start.2 = (s32[512,1]{0,1:T(1,128)S(1)}, s32[512,1]{0,1:T(1,128)}, u32[]{:S(2)}) copy-start(s32[512,1]{0,1:T(1,128)} %param.17) | copy-start | bytes 6148
  25.6 77.4 %copy-start.9 = (s32[512,1,8]{0,2,1:T(8,128)S(1)}, s32[512,1,8]{0,2,1:T(8,128)}, u32[]{:S(2)}) copy-start(s32[512,1,8]{0,2,1:T(8,128)} %param.18) | copy-start | bytes 49156
  25.6 79.7 %copy-start.10 = (s32[2,128]{1,0:T(2,128)S(1)}, s32[2,128]{1,0:T(2,128)}, u32[]{:S(2)}) copy-start(s32[2,128]{1,0:T(2,128)} %param.21) | copy-start | bytes 3076
  94.0 55.8 %all-to-all-start = ((bf16[32,2,1,128,128]{4,3,1,2,0:T(8,128)(2,1)}), bf16[32,2,1,128,128]{4,3,1,2,0:T(8,128)(2,1)S(1)}, u32[]{:S(2)}, u32[]{:S(2)}) async-start(bf16[32,2,1,128,128]{4,3,1,2,0:T(8,128)(2,1)} %get-tuple-element.56), calls=%async_computation | async-start | bytes 4194304 | tf_op jit(solution)/shard_map/all_to_all | solution.py:80
  157.0 212.4 %copy-start.6 = (bf16[256,128]{1,0:T(8,128)(2,1)}, bf16[256,128]{1,0:T(8,128)(2,1)S(1)}, u32[]{:S(2)}) copy-start(bf16[256,128]{1,0:T(8,128)(2,1)S(1)} %convolution_convert_fusion.1) | copy-start | bytes 196612
  218.2 151.2 %copy-start.7 = (bf16[256,128]{1,0:T(8,128)(2,1)}, bf16[256,128]{1,0:T(8,128)(2,1)S(1)}, u32[]{:S(2)}) copy-start(bf16[256,128]{1,0:T(8,128)(2,1)S(1)} %convolution_convert_fusion.2) | copy-start | bytes 196612
  369.5 3.6 copy-start.5
  376.7 3.4 copy-start.4
Sparse Core Ops, SparseCore 0:
  10.6 88.8 all-gather.10
  101.3 36.6 all-gather.4
  140.6 73.5 all-gather.8
  216.6 141.2 all-gather.6
where the time goes:
time: 392 us; the launch traced here: 391 us
  waiting for transfers between devices  234 us (60%)
  blocking collectives  68.4 us (17%)
  matrix products  33.7 us (9%)
  local copies, waits for them, and re-layouts  25.9 us (7%)
  between operations  14.2 us (4%)
  starting transfers between devices  7.63 us (2%)
  other arithmetic  7.57 us (2%)
    all_gather x1, waiting for transfers between devices, shards(): lax.all_gather(w_query, 'req', axis=0, tiled=True)  140 us
    all_to_all x1, blocking collectives, shards(): lax.all_to_all(pack(doc_values), 'req', split_axis=0, concat_axis=0, tile...  68.4 us
    all_gather x1, waiting for transfers between devices, shards(): lax.all_gather(w_key, 'req', axis=0, tiled=True)  56.9 us
    all_to_all x1, waiting for transfers between devices, shards(): lax.all_to_all(pack(doc_keys), 'req', split_axis=0, concat_axis=0, tiled=...  34.6 us
    dot_general x3, matrix products, shards(): jnp.dot(whole, piece, preferred_element_type=jnp.float32)  19.8 us
  transfers between devices with their start and end apart: 5, of which 3 were waited for; matrix products, arithmetic and copies ran while one was open for 10% of the time, Pallas kernels for 0%

commit v1 on v0

--- a/solution.py
+++ b/solution.py
@@ -3,6 +3,8 @@
 import jax
 import jax.numpy as jnp
 from jax import lax
+from jax.experimental import pallas as pl
+from jax.experimental.pallas import tpu as pltpu
 from jax.sharding import PartitionSpec as P
 
 QH = 64
@@ -27,7 +29,7 @@
     return result.astype(jnp.bfloat16).reshape(block_queries.shape[0], -1)
 
 
-def shards(
+def general(
     hidden,
     w_query,
     w_key,
@@ -132,6 +134,595 @@
     )
 
 
+MESH = pl.DeviceIdType.MESH
+NX, NZ, NY = 4, 8, 4
+COLS = 256
+CHUNKS = 5
+
+
+def exchange_kernel(
+    tab,
+    exsel,
+    hid,
+    dk,
+    dv,
+    wq,
+    wk,
+    wv,
+    q_out,
+    nk_out,
+    nv_out,
+    docs_out,
+    hg,
+    wg,
+    part,
+    r1,
+    r2,
+    xs,
+    xr,
+    ex,
+    zr,
+    own_sem,
+    hx_s,
+    hx_r,
+    hy_s,
+    hy_r,
+    hs_s,
+    hs_r,
+    w_s,
+    w_r,
+    r1_s,
+    r1_r,
+    r2_s,
+    r2_r,
+    dx_s,
+    dx_r,
+    dz_s,
+    dz_r,
+    de_s,
+    de_r,
+    out_sem,
+):
+    r = lax.axis_index("req")
+    h = lax.axis_index("head")
+    z, x = r // NX, lax.rem(r, NX)
+    y, c = h // 2, lax.rem(h, 2)
+
+    def at_x(k):
+        return lax.rem(x + k, NX)
+
+    def at_z(k):
+        return lax.rem(z + k, NZ)
+
+    def dev_x(k):
+        return (z * NX + at_x(k), h)
+
+    def dev_z(k):
+        return (at_z(k) * NX + x, h)
+
+    def head_y(k):
+        return lax.rem(y + k, NY) * 2 + c
+
+    def dev_y(k):
+        return (r, head_y(k))
+
+    sibling = (r, y * 2 + 1 - c)
+
+    def send(src, dst, s, d, device):
+        return pltpu.make_async_remote_copy(
+            src_ref=src, dst_ref=dst, send_sem=s, recv_sem=d, device_id=device, device_id_type=MESH
+        )
+
+    own = []
+    for n in range(4):
+        own.append(
+            pltpu.make_async_copy(
+                wq.at[:, pl.ds(n * COLS, COLS)], wg.at[n, pl.ds(z * 256, 256)], own_sem.at[n]
+            )
+        )
+    own.append(
+        pltpu.make_async_copy(wk, wg.at[4, pl.ds(z * 256, 256), pl.ds(0, HD)], own_sem.at[4])
+    )
+    own.append(
+        pltpu.make_async_copy(wv, wg.at[4, pl.ds(z * 256, 256), pl.ds(HD, HD)], own_sem.at[5])
+    )
+    for copy in own:
+        copy.start()
+
+    barrier = pltpu.get_barrier_semaphore()
+    for k in range(1, NX):
+        pl.semaphore_signal(barrier, inc=1, device_id=dev_x(k), device_id_type=MESH)
+    for k in range(1, NZ):
+        pl.semaphore_signal(barrier, inc=1, device_id=dev_z(k), device_id_type=MESH)
+    for k in (1, 3):
+        pl.semaphore_signal(barrier, inc=1, device_id=dev_y(k), device_id_type=MESH)
+    pl.semaphore_signal(barrier, inc=1, device_id=sibling, device_id_type=MESH)
+    pl.semaphore_wait(barrier, 13)
+
+    started = []
+
+    def go(copy):
+        copy.start()
+        started.append(copy)
+        return copy
+
+    def h_at(row_x, head):
+        return hg.at[
+            pl.ds(pl.multiple_of(row_x * 256, 256), 256),
+            pl.ds(pl.multiple_of(head * 256, 256), 256),
+        ]
+
+    hx = []
+    for k in range(1, NX):
+        cols = pl.ds(pl.multiple_of(at_x(k) * 256, 256), 256)
+        hx.append(
+            go(send(hid.at[:, cols], h_at(x, h), hx_s.at[k - 1], hx_r.at[k - 1], dev_x(k)))
+        )
+    own_h = pltpu.make_async_copy(
+        hid.at[:, pl.ds(pl.multiple_of(x * 256, 256), 256)], h_at(x, h), own_sem.at[6]
+    )
+    own_h.start()
+
+    def w_step(n, s):
+        pair = []
+        for way in range(2):
+            if s > 1:
+                w_copies[(n, s - 1, way)].wait_recv()
+        for way in range(2):
+            back = (NZ - (s - 1)) if way == 0 else (s - 1)
+            block = at_z(back) * 256
+            if s < 4:
+                rows = pl.ds(pl.multiple_of(block, 256), 256)
+            else:
+                rows = pl.ds(pl.multiple_of(block + 128 * way, 128), 128)
+            ref = wg.at[n, rows]
+            i = (n * 4 + s - 1) * 2 + way
+            pair.append(go(send(ref, ref, w_s.at[i], w_r.at[i], dev_z(1 if way == 0 else NZ - 1))))
+        w_copies[(n, s, 0)], w_copies[(n, s, 1)] = pair
+
+    w_copies = {}
+
+    def w_slot(t):
+        for n in range(CHUNKS):
+            s = t - n
+            if 1 <= s <= 4:
+                if s == 1:
+                    own[n].wait()
+                    if n == 4:
+                        own[5].wait()
+                w_step(n, s)
+
+    def w_finish(n):
+        for way in range(2):
+            w_copies[(n, 4, way)].wait_recv()
+
+    w_slot(1)
+
+    def pack(zt, carry):
+        for k in range(NX):
+            target = zt * NX + at_x(k)
+            for rank in range(2):
+                index = tab[target * 2 + rank]
+                keys, values = dk[index], dv[index]
+                if k == 0:
+                    xr[x, rank, zt, 0] = keys
+                    xr[x, rank, zt, 1] = values
+                else:
+                    xs[k - 1, rank, zt, 0] = keys
+                    xs[k - 1, rank, zt, 1] = values
+        return carry
+
+    lax.fori_loop(0, NZ, pack, 0)
+
+    def send_docs_x(rank):
+        copies = []
+        for k in range(1, NX):
+            i = rank * 3 + k - 1
+            copies.append(
+                go(send(xs.at[k - 1, rank], xr.at[x, rank], dx_s.at[i], dx_r.at[i], dev_x(k)))
+            )
+        return copies
+
+    w_slot(2)
+    for copy in hx:
+        copy.wait_recv()
+    own_h.wait()
+
+    def h_cols(head, rows=slice(0, 1024)):
+        return hg.at[
+            pl.ds(rows.start, rows.stop - rows.start), pl.ds(pl.multiple_of(head * 256, 256), 256)
+        ]
+
+    hy, hs = [], []
+    for way, k in ((0, 1), (1, 3)):
+        hy.append(go(send(h_cols(h), h_cols(h), hy_s.at[way], hy_r.at[way], dev_y(k))))
+    hs.append(go(send(h_cols(h), h_cols(h), hs_s.at[0], hs_r.at[0], sibling)))
+    docs_x = send_docs_x(0)
+    w_slot(3)
+    w_slot(4)
+    for copy in hy:
+        copy.wait_recv()
+    top, bottom = slice(0, 512), slice(512, 1024)
+    left, right = head_y(3), head_y(1)
+    hy2 = [
+        go(send(h_cols(left, top), h_cols(left, top), hy_s.at[2], hy_r.at[2], dev_y(1))),
+        go(send(h_cols(right, bottom), h_cols(right, bottom), hy_s.at[3], hy_r.at[3], dev_y(3))),
+    ]
+    hs.append(go(send(h_cols(left), h_cols(left), hs_s.at[1], hs_r.at[1], sibling)))
+    hs.append(go(send(h_cols(right), h_cols(right), hs_s.at[2], hs_r.at[2], sibling)))
+    w_slot(5)
+    for copy in hy2:
+        copy.wait_recv()
+    far = head_y(2)
+    hs.append(go(send(h_cols(far), h_cols(far), hs_s.at[3], hs_r.at[3], sibling)))
+    for copy in hs:
+        copy.wait_recv()
+
+    def product(n, k):
+        block = lax.rem(x + k, NX)
+        rows = pl.ds(pl.multiple_of(block * 256, 256), 256)
+        part[n, block] = jnp.dot(hg[rows, :], wg[n], preferred_element_type=jnp.float32)
+
+    r1_copies, r2_copies = {}, {}
+
+    def multiply(n):
+        w_finish(n)
+        product(n, 2)
+        far_x = at_x(2)
+        r1_copies[n] = [
+            go(
+                send(
+                    part.at[n, far_x, pl.ds(128 * way, 128)],
+                    r1.at[n, way],
+                    r1_s.at[n * 2 + way],
+                    r1_r.at[n * 2 + way],
+                    dev_x(1 if way == 0 else 3),
+                )
+            )
+            for way in range(2)
+        ]
+
+        def rest(k, carry):
+            product(n, k)
+            return carry
+
+        lax.fori_loop(3, 6, rest, 0)
+
+    def second(n):
+        for copy in r1_copies[n]:
+            copy.wait_recv()
+        part[n, at_x(1), pl.ds(0, 128)] = part[n, at_x(1), pl.ds(0, 128)] + r1[n, 0]
+        part[n, at_x(3), pl.ds(128, 128)] = part[n, at_x(3), pl.ds(128, 128)] + r1[n, 1]
+        r2_copies[n] = [
+            go(
+                send(
+                    part.at[n, at_x(1 if way == 0 else 3)],
+                    r2.at[n, way],
+                    r2_s.at[n * 2 + way],
+                    r2_r.at[n * 2 + way],
+                    dev_x(1 if way == 0 else 3),
+                )
+            )
+            for way in range(2)
+        ]
+
+    def third(n):
+        for copy in r2_copies[n]:
+            copy.wait_recv()
+        total = (part[n, x] + r2[n, 0] + r2[n, 1]).astype(jnp.bfloat16)
+        if n < 4:
+            q_out[:, pl.ds(n * COLS, COLS)] = total
+        else:
+            nk_out[...] = total[:, :HD]
+            nv_out[...] = total[:, HD:]
+
+    multiply(0)
+    w_slot(6)
+    docs_x1 = send_docs_x(1)
+    multiply(1)
+    second(0)
+    w_slot(7)
+    multiply(2)
+    second(1)
+    third(0)
+    w_slot(8)
+
+    for copy in docs_x:
+        copy.wait_recv()
+    docs_z = []
+    for k in (4, 3, 5, 2, 6, 1, 7):
+        docs_z.append(
+            go(
+                send(
+                    xr.at[:, 0, at_z(k)],
+                    zr.at[z, pl.ds(0, 4)],
+                    dz_s.at[k - 1],
+                    dz_r.at[k - 1],
+                    dev_z(k),
+                )
+            )
+        )
+    own_z = pltpu.make_async_copy(xr.at[:, 0, z], zr.at[z, pl.ds(0, 4)], own_sem.at[7])
+    own_z.start()
+
+    multiply(3)
+    second(2)
+    third(1)
+    multiply(4)
+    second(3)
+    third(2)
+
+    for copy in docs_x1:
+        copy.wait_recv()
+
+    def extra(zt, carry):
+        chosen = exsel[zt]
+        ex[zt] = xr[chosen, 1, zt]
+        return carry
+
+    lax.fori_loop(0, NZ, extra, 0)
+    docs_e = []
+    for k in (4, 3, 5, 2, 6, 1, 7):
+        docs_e.append(
+            go(send(ex.at[at_z(k)], zr.at[z, 4], de_s.at[k - 1], de_r.at[k - 1], dev_z(k)))
+        )
+    own_e = pltpu.make_async_copy(ex.at[z], zr.at[z, 4], own_sem.at[8])
+    own_e.start()
+
+    second(4)
+    third(3)
+    third(4)
+    own_z.wait()
+    own_e.wait()
+    for copy in docs_z:
+        copy.wait_recv()
+    for copy in docs_e:
+        copy.wait_recv()
+    result = pltpu.make_async_copy(zr, docs_out, out_sem)
+    result.start()
+    for copy in started:
+        copy.wait_send()
+    result.wait()
+
+
+def exchange(tab, exsel, hid, dk, dv, wq, wk, wv):
+    vmem = pl.BlockSpec(memory_space=pltpu.VMEM)
+    smem = pl.BlockSpec(memory_space=pltpu.SMEM)
+    anym = pl.BlockSpec(memory_space=pl.ANY)
+    dma = pltpu.SemaphoreType.DMA
+    bf16, f32 = jnp.bfloat16, jnp.float32
+    return pl.pallas_call(
+        exchange_kernel,
+        out_shape=(
+            jax.ShapeDtypeStruct((256, 1024), bf16),
+            jax.ShapeDtypeStruct((256, HD), bf16),
+            jax.ShapeDtypeStruct((256, HD), bf16),
+            jax.ShapeDtypeStruct((NZ, 5, 2, 128, HD), bf16),
+        ),
+        in_specs=[smem, smem, vmem, vmem, vmem, anym, anym, anym],
+        out_specs=(vmem, vmem, vmem, anym),
+        scratch_shapes=[
+            pltpu.VMEM((1024, 2048), bf16),
+            pltpu.VMEM((CHUNKS, 2048, COLS), bf16),
+            pltpu.VMEM((CHUNKS, NX, 256, COLS), f32),
+            pltpu.VMEM((CHUNKS, 2, 128, COLS), f32),
+            pltpu.VMEM((CHUNKS, 2, 256, COLS), f32),
+            pltpu.VMEM((3, 2, NZ, 2, 128, HD), bf16),
+            pltpu.VMEM((NX, 2, NZ, 2, 128, HD), bf16),
+            pltpu.VMEM((NZ, 2, 128, HD), bf16),
+            pltpu.VMEM((NZ, 5, 2, 128, HD), bf16),
+            dma((9,)),
+            dma((3,)),
+            dma((3,)),
+            dma((4,)),
+            dma((4,)),
+            dma((4,)),
+            dma((4,)),
+            dma((40,)),
+            dma((40,)),
+            dma((10,)),
+            dma((10,)),
+            dma((10,)),
+            dma((10,)),
+            dma((6,)),
+            dma((6,)),
+            dma((7,)),
+            dma((7,)),
+            dma((7,)),
+            dma((7,)),
+            dma,
+        ],
+        compiler_params=pltpu.CompilerParams(
+            collective_id=0, has_side_effects=True, vmem_limit_bytes=48 * 2**20
+        ),
+    )(tab, exsel, hid, dk, dv, wq, wk, wv)
+
+
+def attention_kernel(
+    where, rows, ids, kept, counts, q, nk, nv, docs, out, keys, values, bias
+):
+    request, pair = pl.program_id(0), pl.program_id(1)
+    span = SLOTS * BLK
+
+    @pl.when((request == 0) & (pair == 0))
+    def _():
+        hot = (ids[...] == lax.broadcasted_iota(jnp.int32, (2 * NDOC, 512), 1)).astype(jnp.bfloat16)
+        blocks = jnp.dot(
+            hot, kept[...].astype(jnp.float32).astype(jnp.bfloat16), preferred_element_type=jnp.float32
+        )
+        spread = (
+            lax.broadcasted_iota(jnp.int32, (SLOTS, span), 1) // BLK
+            == lax.broadcasted_iota(jnp.int32, (SLOTS, span), 0)
+        ).astype(jnp.bfloat16)
+        block = jnp.dot(
+            blocks.astype(jnp.bfloat16), spread, preferred_element_type=jnp.float32
+        ).astype(jnp.int32)
+        count = jnp.dot(
+            hot,
+            jnp.broadcast_to(counts[...], (512, span)).astype(jnp.float32).astype(jnp.bfloat16),
+            preferred_element_type=jnp.float32,
+        ).astype(jnp.int32)
+        token = lax.broadcasted_iota(jnp.int32, (2 * NDOC, span), 1)
+        ref = lax.broadcasted_iota(jnp.int32, (2 * NDOC, span), 0)
+        position = lax.rem(ref, NDOC) * (DOC_BLKS * BLK) + block * BLK + lax.rem(token, BLK)
+        dead = (token // BLK >= count).astype(jnp.int32)
+        first = ref < NDOC
+
+        def compare(k, dead):
+            row = jnp.where(first, rows[0, k], rows[1, k])
+            return dead | (position == row).astype(jnp.int32)
+
+        dead = lax.fori_loop(0, 128, compare, dead)
+        shut = jnp.where(dead > 0, -jnp.inf, 0.0)
+        for i in range(2):
+            for j in range(NDOC):
+                bias[i, :, pl.ds(j * span, span)] = shut[i * NDOC + j : i * NDOC + j + 1]
+            bias[i, :, pl.ds(NDOC * span, 128)] = jnp.zeros((1, 128), jnp.float32)
+
+    @pl.when(pair == 0)
+    def _():
+        for j in range(NDOC):
+            slot = where[request * NDOC + j]
+            keys[pl.ds(j * span, span)] = docs[slot, 0]
+            values[pl.ds(j * span, span)] = docs[slot, 1]
+        keys[pl.ds(NDOC * span, 128)] = nk[...]
+        values[pl.ds(NDOC * span, 128)] = nv[...]
+
+    scale = 1.0 / math.sqrt(HD)
+    for g in range(2):
+        cols = pl.ds(g * HD, HD)
+        scores = lax.dot_general(
+            q[:, cols], keys[...], (((1,), (1,)), ((), ())), preferred_element_type=jnp.float32
+        )
+        scores = scores * scale + bias[request]
+        peak = jnp.max(scores, axis=-1, keepdims=True)
+        weights = jnp.exp(scores - peak)
+        probs = (weights / jnp.sum(weights, axis=-1, keepdims=True)).astype(jnp.bfloat16)
+        out[:, cols] = jnp.dot(probs, values[...], preferred_element_type=jnp.float32).astype(
+            jnp.bfloat16
+        )
+
+
+def attention(where, rows, ids, kept, counts, q, nk, nv, docs):
+    smem = pl.BlockSpec(memory_space=pltpu.SMEM)
+    vmem = pl.BlockSpec(memory_space=pltpu.VMEM)
+    context = NDOC * SLOTS * BLK + 128
+    return pl.pallas_call(
+        attention_kernel,
+        grid=(2, 4),
+        out_shape=jax.ShapeDtypeStruct((256, 1024), jnp.bfloat16),
+        in_specs=[
+            smem,
+            smem,
+            vmem,
+            vmem,
+            vmem,
+            pl.BlockSpec((128, 256), lambda i, p: (i, p)),
+            pl.BlockSpec((128, HD), lambda i, p: (i, 0)),
+            pl.BlockSpec((128, HD), lambda i, p: (i, 0)),
+            vmem,
+        ],
+        out_specs=pl.BlockSpec((128, 256), lambda i, p: (i, p)),
+        scratch_shapes=[
+            pltpu.VMEM((context, HD), jnp.bfloat16),
+            pltpu.VMEM((context, HD), jnp.bfloat16),
+            pltpu.VMEM((2, 1, context), jnp.float32),
+        ],
+        compiler_params=pltpu.CompilerParams(vmem_limit_bytes=48 * 2**20),
+    )(where, rows, ids, kept, counts, q, nk, nv, docs)
+
+
+def shards(
+    hidden,
+    w_query,
+    w_key,
+    w_value,
+    doc_keys,
+    doc_values,
+    slot_counts,
+    kept_blocks,
+    doc_ids,
+    doc_place,
+    recompute_rows,
+):
+    owners = lax.axis_size("req")
+    mine = lax.axis_index("req")
+    refs = 2 * NDOC
+    my_z, my_x = mine // NX, lax.rem(mine, NX)
+    flat = doc_ids.reshape(-1)
+    placed = jnp.sum(
+        jnp.where(flat[:, None] == jnp.arange(512, dtype=jnp.int32)[None, :], doc_place[None, :], 0),
+        axis=1,
+    ).reshape(owners, refs)
+    owner_all, local_all = placed // 16, placed % 16
+    order = jnp.arange(refs, dtype=jnp.int32)
+    spare = refs * 16
+    key = jnp.where(owner_all == mine, order[None, :] * 16 + local_all, spare)
+    first = jnp.min(key, axis=1)
+    second = jnp.min(jnp.where(key > first[:, None], key, spare), axis=1)
+    tab = jnp.stack([first % 16, second % 16], axis=1).reshape(-1)
+    held = jnp.sum(
+        (owner_all[:, None, :] == jnp.arange(owners, dtype=jnp.int32)[None, :, None]).astype(jnp.int32),
+        axis=2,
+    )
+    twice = (held > 1).reshape(owners, NZ, NX)
+    crowded = jnp.any(jnp.sum(twice.astype(jnp.int32), axis=2) > 1)
+    my_twice = lax.dynamic_index_in_dim(twice, my_z, 1, False)
+    choice = jnp.max(jnp.where(my_twice, jnp.arange(NX, dtype=jnp.int32)[None, :], 0), axis=1)
+    exsel = lax.dynamic_index_in_dim(choice.reshape(NZ, NX), my_x, 1, False)
+    own_owner = lax.dynamic_index_in_dim(owner_all, mine, 0, False)
+    later = jnp.any(
+        (own_owner[:, None] == own_owner[None, :]) & (order[None, :] < order[:, None]), axis=1
+    )
+    where = (own_owner // NX) * 5 + jnp.where(later, 4, own_owner % NX)
+    ids = lax.dynamic_slice_in_dim(doc_ids, mine * 2, 2, 0).reshape(refs, 1)
+
+    def fast():
+        q, nk, nv, docs = exchange(
+            tab,
+            exsel,
+            hidden.reshape(256, -1),
+            doc_keys.reshape(16, 128, HD),
+            doc_values.reshape(16, 128, HD),
+            w_query,
+            w_key,
+            w_value,
+        )
+        attended = attention(
+            where,
+            recompute_rows,
+            ids,
+            kept_blocks.reshape(512, SLOTS),
+            slot_counts,
+            q,
+            nk,
+            nv,
+            docs.reshape(NZ * 5, 2, 128, HD),
+        )
+        return (
+            attended.reshape(2, 128, 1024),
+            nk.reshape(2, 128, HD),
+            nv.reshape(2, 128, HD),
+        )
+
+    def slow():
+        return general(
+            hidden,
+            w_query,
+            w_key,
+            w_value,
+            doc_keys,
+            doc_values,
+            slot_counts,
+            kept_blocks,
+            doc_ids,
+            doc_place,
+            recompute_rows,
+        )
+
+    return lax.cond(crowded, slow, fast)
+
+
 def solution(mesh):
     return jax.shard_map(
         shards,

time: 392 us -> 183 us (0.47)
  waiting for transfers between devices: 234 us -> 0 us
  Pallas kernels: 0 us -> 155 us
  blocking collectives: 68.4 us -> 0 us
  matrix products: 33.7 us -> 0 us
  local copies, waits for them, and re-layouts: 25.9 us -> 7.27 us
  starting transfers between devices: 7.63 us -> 0 us
  other arithmetic: 7.57 us -> 2.99 us
    all_gather x4 -> x0, waiting for transfers between devices: 197 us -> none  [the longest x1 140 us: shards(): lax.all_gather(w_query, 'req', axis=0, tiled=True)]
    pallas_call x0 -> x2, Pallas kernels: none -> 155 us  [the longest x1 139 us: exchange(): pl.pallas_call(exchange_kernel, out_shape=(jax.ShapeDtypeStruct((256, 102...]
    all_to_all x1 -> x0, blocking collectives: 68.4 us -> none  [shards(): lax.all_to_all(pack(doc_values), 'req', split_axis=0, concat_axis=0, tile...]
    all_to_all x1 -> x0, waiting for transfers between devices: 34.6 us -> none  [shards(): lax.all_to_all(pack(doc_keys), 'req', split_axis=0, concat_axis=0, tiled=...]
    dot_general x5 -> x0, matrix products: 26.7 us -> none  [the longest x3 19.8 us: shards(): jnp.dot(whole, piece, preferred_element_type=jnp.float32)]
    gather x10 -> x0, local copies, waits for them, and re-layouts: 17.5 us -> none  [the longest x2 6.94 us: shards(): placed = doc_place[doc_ids]]
    all_to_all x1 -> x0, starting transfers between devices: 7.48 us -> none  [shards(): lax.all_to_all(pack(doc_keys), 'req', split_axis=0, concat_axis=0, tiled=...]
    sub x2 -> x0, matrix products: 6.95 us -> none  [attend(): weights = jnp.exp(scores - peak)]
  transfers between devices with their start and end apart: 5 -> 0, of which waited for: 3 -> 0; matrix products, arithmetic and copies ran while one was open for 10% -> 0% of each run, Pallas kernels for 0% -> 0%
where the time goes in v1:
time: 183 us; the launch traced here: 181 us
  Pallas kernels  155 us (85%)
  between operations  14.7 us (8%)
  local copies, waits for them, and re-layouts  7.27 us (4%)
  other arithmetic  2.99 us (2%)
    pallas_call x1, Pallas kernels, exchange(): pl.pallas_call(exchange_kernel, out_shape=(jax.ShapeDtypeStruct((256, 102...  139 us
    pallas_call x1, Pallas kernels, attention(): pl.pallas_call(attention_kernel, grid=(2, 4), out_shape=jax.ShapeDtypeStr...  16.5 us

profile of v1, /device:TPU:1, one launch (start us, length us, event | category | flops | bytes accessed | tf_op | source)
XLA Modules:
  0.0 180.5 jit_solution(12750388773560512070)
XLA Ops:
  7.2 0.8 copy.100
  8.0 1.2 select_reduce_fusion.1
  9.3 0.1 fusion.93
  9.4 0.6 convert_reduce_fusion.2
  10.0 0.1 copy.101
  10.2 0.2 dynamic-slice_reduce_fusion
  10.4 0.2 fusion.86
  10.7 0.2 fusion.83
  10.9 0.1 copy.102
  11.0 0.1 reshape.576
  11.1 0.8 constant_dynamic-slice_fusion.3
  11.8 0.1 copy.103
  11.9 0.1 reshape.578
  12.0 0.6 compare_reduce_fusion.2
  13.3 159.1 %conditional.1 = (bf16[256,128]{1,0:T(8,128)(2,1)S(1)}, bf16[256,128]{1,0:T(8,128)(2,1)S(1)}, bf16[2,128,1024]{2,1,0:T(8,128)(2,1)}) conditional(s32[]{:T(128)} %convert_element_type.42, (s32[512,1,8]{0,2,1:T(8,128)}, bf16[2,128,1024]{2,1,0:T(8,128)(2,1)}, bf16[16,1,128,128]{3,2,1,0:T(8,128)(2,1)}, bf16[16,1,128,128]{3,2,1,0:T(8,128)(2,1)}, ...), branch_computations={%region_8.9_spmd, %region_9.19_spmd} | conditional | flops 8842248192 | bytes 167148928 | solution.py:723
  13.3 139.0 %branch_0_fun.2 = (bf16[256,1024]{1,0:T(8,128)(2,1)S(1)}, bf16[256,128]{1,0:T(8,128)(2,1)S(1)}, bf16[256,128]{1,0:T(8,128)(2,1)S(1)}, bf16[8,5,2,128,128]{4,3,2,1,0:T(8,128)(2,1)S(1)}) custom-call(s32[64]{0:T(128)S(1)} %get-tuple-element.66.tab, s32[8]{0:T(128)S(1)} %get-tuple-element.73.exsel, bf16[256,1024]{1,0:T(8,128)(2,1)} %bitcast.137, ...), custom_call_target="tpu_custom_call" | custom-call | tf_op jit(solution)/shard_map/cond/branch_0_fun/pallas_call | solution.py:494
  152.4 0.8 copy-done
  153.2 0.8 copy.104
  154.0 0.8 copy.108.counts
  154.8 0.1 copy.107.ids
  154.9 1.0 copy-done.1
  156.0 16.5 %branch_0_fun.3 = bf16[256,1024]{1,0:T(8,128)(2,1)} custom-call(s32[32]{0:T(128)S(1)} %get-tuple-element.61.where, s32[2,128]{1,0:T(2,128)} %get-tuple-element.62.rows, s32[32,1]{1,0:T(8,128)S(1)} %copy.107.ids, s32[512,8]{1,0:T(8,128)S(1)} %bitcast.125, s32[512,1]{1,0:T(8,128)S(1)} %copy.108.counts, bf16[256,1024]{1,0:T(8,128)(2,1)S(1)} %copy-done.1, ...), custom_call_target="tpu_custom_call" | custom-call | tf_op jit(solution)/shard_map/cond/branch_0_fun/pallas_call | solution.py:610
  172.4 0.6 copy.156
  173.1 0.6 copy.157
  (13 shorter events, 0.3 us)
Async XLA Ops:
  152.4 0.8 copy-start
  154.9 1.0 copy-start.1

commit v2 on v1

v2 whole, which is shorter than its diff:
```python
import math

import jax
import jax.numpy as jnp
from jax import lax
from jax.experimental import pallas as pl
from jax.experimental.pallas import tpu as pltpu
from jax.sharding import PartitionSpec as P

QH = 64
KVH = 8
HD = 128
BLK = 16
DOC_BLKS = 16
SLOTS = 8
NDOC = 16


def attend(block_queries, context_keys, context_values, live, scale):
    scores = (
        jnp.einsum("rgd,kd->rgk", block_queries, context_keys, preferred_element_type=jnp.float32)
        * scale
    )
    scores = jnp.where(live[None, None, :], scores, -jnp.inf)
    peak = jnp.max(scores, axis=-1, keepdims=True)
    weights = jnp.exp(scores - peak)
    probs = (weights / jnp.sum(weights, axis=-1, keepdims=True)).astype(jnp.bfloat16)
    result = jnp.einsum("rgk,kd->rgd", probs, context_values, preferred_element_type=jnp.float32)
    return result.astype(jnp.bfloat16).reshape(block_queries.shape[0], -1)


def general(
    queries,
    keys_new,
    values_new,
    doc_keys,
    doc_values,
    slot_counts,
    kept_blocks,
    doc_ids,
    doc_place,
    recompute_rows,
):
    req_here, rows_req, heads_here = 2, queries.shape[0] // 2, 1
    group = QH // KVH
    span = SLOTS * BLK
    scale = 1.0 / math.sqrt(HD)
    owners = lax.axis_size("req")
    mine = lax.axis_index("req")
    docs_here = doc_keys.shape[0]
    refs = req_here * NDOC
    capacity = 2 * (refs // owners)
    placed = doc_place[doc_ids]
    owner_all = (placed // docs_here).reshape(owners, refs)
    local_all = (placed % docs_here).reshape(owners, refs)
    order = jnp.arange(refs, dtype=jnp.int32)
    earlier = (owner_all[:, :, None] == owner_all[:, None, :]) & (
        order[None, None, :] < order[None, :, None]
    )
    rank = jnp.sum(earlier.astype(jnp.int32), axis=2)
    slot_ids = jnp.arange(capacity, dtype=jnp.int32)
    match = (
        (owner_all == mine)[:, :, None] & (rank[:, :, None] == slot_ids[None, None, :])
    ).astype(jnp.int32)
    picked = jnp.sum(match * local_all[:, :, None], axis=1)
    used = jnp.sum(match, axis=1) > 0

    def pack(cache):
        selected = cache[picked]
        return jnp.where(used[:, :, None, None, None], selected, jnp.zeros_like(selected))

    got_keys = lax.all_to_all(pack(doc_keys), "req", split_axis=0, concat_axis=0, tiled=True)
    got_values = lax.all_to_all(pack(doc_values), "req", split_axis=0, concat_axis=0, tiled=True)
    own_owner = lax.dynamic_index_in_dim(owner_all, mine, 0, False)
    own_rank = lax.dynamic_index_in_dim(rank, mine, 0, False)
    where_row = own_owner * capacity + own_rank
    tail = got_keys.shape[2:]
    fetched_keys = got_keys.reshape((owners * capacity,) + tail)[where_row].reshape(
        (req_here, NDOC) + tail
    )
    fetched_values = got_values.reshape((owners * capacity,) + tail)[where_row].reshape(
        (req_here, NDOC) + tail
    )
    queries = queries.reshape(req_here, rows_req, heads_here, group, HD)
    keys_new = keys_new.reshape(req_here, rows_req, heads_here, HD)
    values_new = values_new.reshape(req_here, rows_req, heads_here, HD)
    my_ids = lax.dynamic_slice_in_dim(doc_ids, mine * req_here, req_here, 0)
    offsets = jnp.arange(NDOC, dtype=jnp.int32)[:, None, None] * (DOC_BLKS * BLK)
    inner = jnp.arange(BLK, dtype=jnp.int32)[None, None, :]
    slot_index = jnp.arange(SLOTS, dtype=jnp.int32)[None, :, None]
    block_rows = 128
    request_outputs = []
    for request in range(req_here):
        ids = my_ids[request]
        positions = recompute_rows[request]
        blocks = kept_blocks[ids, 0]
        count_here = slot_counts[ids, 0]
        key_pos = (offsets + blocks[:, :, None] * BLK + inner).reshape(-1)
        valid = (slot_index < count_here[:, None, None]) & (inner >= 0)
        replaced = jnp.any(key_pos[:, None] == positions[None, :], axis=1)
        live = jnp.concatenate(
            [valid.reshape(-1) & jnp.logical_not(replaced), jnp.ones((rows_req,), bool)]
        )
        context_keys = jnp.concatenate(
            [fetched_keys[request, :, 0].reshape(NDOC * span, HD), keys_new[request, :, 0]], axis=0
        )
        context_values = jnp.concatenate(
            [fetched_values[request, :, 0].reshape(NDOC * span, HD), values_new[request, :, 0]],
            axis=0,
        )
        query_blocks = queries[request, :, 0].reshape(rows_req // block_rows, block_rows, group, HD)
        result = lax.map(
            lambda block_queries: attend(block_queries, context_keys, context_values, live, scale),
            query_blocks,
        )
        head_outputs = result.reshape(rows_req, group * HD)
        request_outputs.append(head_outputs)
    return jnp.stack(request_outputs, axis=0)


MESH = pl.DeviceIdType.MESH
NX, NZ, NY = 4, 8, 4
COLS = 256
CHUNKS = 5


def exchange_kernel(
    rows,
    place,
    ids,
    kept,
    counts,
    hid,
    dk_in,
    dv_in,
    wq,
    wk,
    wv,
    out,
    q_out,
    nk_out,
    nv_out,
    flag,
    placed,
    table,
    tab,
    dk,
    dv,
    keys,
    values,
    bias,
    points,
    peaks,
    hg,
    wg,
    part,
    r1,
    r2,
    xs,
    xr,
    xr1,
    ex,
    zr,
    own_sem,
    hx_s,
    hx_r,
    hy_s,
    hy_r,
    hs_s,
    hs_r,
    w_s,
    w_r,
    r1_s,
    r1_r,
    r2_s,
    r2_r,
    dx_s,
    dx_r,
    dz_s,
    dz_r,
    de_s,
    de_r,
):
    r = lax.axis_index("req")
    h = lax.axis_index("head")
    z, x = r // NX, lax.rem(r, NX)
    y, c = h // 2, lax.rem(h, 2)

    def at_x(k):
        return lax.rem(x + k, NX)

    def at_z(k):
        return lax.rem(z + k, NZ)

    def dev_x(k):
        return (z * NX + at_x(k), h)

    def dev_z(k):
        return (at_z(k) * NX + x, h)

    def head_y(k):
        return lax.rem(y + k, NY) * 2 + c

    def dev_y(k):
        return (r, head_y(k))

    sibling = (r, y * 2 + 1 - c)

    def send(src, dst, s, d, device):
        return pltpu.make_async_remote_copy(
            src_ref=src, dst_ref=dst, send_sem=s, recv_sem=d, device_id=device, device_id_type=MESH
        )

    docs_in = [
        pltpu.make_async_copy(dk_in, dk, own_sem.at[9]),
        pltpu.make_async_copy(dv_in, dv, own_sem.at[10]),
    ]
    own = []
    for n in range(4):
        own.append(
            pltpu.make_async_copy(
                wq.at[:, pl.ds(n * COLS, COLS)], wg.at[n, pl.ds(z * 256, 256)], own_sem.at[n]
            )
        )
    own.append(
        pltpu.make_async_copy(wk, wg.at[4, pl.ds(z * 256, 256), pl.ds(0, HD)], own_sem.at[4])
    )
    own.append(
        pltpu.make_async_copy(wv, wg.at[4, pl.ds(z * 256, 256), pl.ds(HD, HD)], own_sem.at[5])
    )
    for copy in own + docs_in:
        copy.start()

    barrier = pltpu.get_barrier_semaphore()
    for k in range(1, NX):
        pl.semaphore_signal(barrier, inc=1, device_id=dev_x(k), device_id_type=MESH)
    for k in range(1, NZ):
        pl.semaphore_signal(barrier, inc=1, device_id=dev_z(k), device_id_type=MESH)
    for k in (1, 3):
        pl.semaphore_signal(barrier, inc=1, device_id=dev_y(k), device_id_type=MESH)
    pl.semaphore_signal(barrier, inc=1, device_id=sibling, device_id_type=MESH)
    pl.semaphore_wait(barrier, 13)

    started = []

    def go(copy):
        copy.start()
        started.append(copy)
        return copy

    def mask():
        span = SLOTS * BLK
        refs = 2 * NDOC
        hot = (
            lax.broadcasted_iota(jnp.int32, (512, refs), 0)
            == jnp.broadcast_to(ids[pl.ds(r, 1), :], (512, refs))
        ).astype(jnp.float32)
        hot = hot.astype(jnp.bfloat16)

        def whole(a):
            return a.astype(jnp.float32).astype(jnp.bfloat16)

        blocks = jnp.dot(whole(kept[...]), hot, preferred_element_type=jnp.float32)
        spread = whole(
            (
                lax.broadcasted_iota(jnp.int32, (SLOTS, span), 1) // BLK
                == lax.broadcasted_iota(jnp.int32, (SLOTS, span), 0)
            ).astype(jnp.int32)
        )
        across = (((0,), (0,)), ((), ()))
        block = lax.dot_general(
            blocks.astype(jnp.bfloat16), spread, across, preferred_element_type=jnp.float32
        ).astype(jnp.int32)
        held = jnp.dot(
            whole(jnp.broadcast_to(counts[...], (8, 512))), hot, preferred_element_type=jnp.float32
        )
        eighth = jnp.full((8, span), 0.125, jnp.bfloat16)
        count = lax.dot_general(
            held.astype(jnp.bfloat16), eighth, across, preferred_element_type=jnp.float32
        ).astype(jnp.int32)
        token = lax.broadcasted_iota(jnp.int32, (refs, span), 1)
        ref = lax.broadcasted_iota(jnp.int32, (refs, span), 0)
        position = lax.rem(ref, NDOC) * (DOC_BLKS * BLK) + block * BLK + lax.rem(token, BLK)
        dead = (token // BLK >= count).astype(jnp.int32)
        first = ref < NDOC

        def compare(k, dead):
            row = jnp.where(first, rows[0, k], rows[1, k])
            return dead | (position == row).astype(jnp.int32)

        dead = lax.fori_loop(0, 128, compare, dead)
        shut = jnp.where(dead > 0, -jnp.inf, 0.0)
        for i in range(2):
            for j in range(NDOC):
                bias[i, :, pl.ds(j * span, span)] = shut[i * NDOC + j : i * NDOC + j + 1]
            bias[i, :, pl.ds(NDOC * span, 128)] = jnp.zeros((1, 128), jnp.float32)

    def h_at(row_x, head):
        return hg.at[
            pl.ds(pl.multiple_of(row_x * 256, 256), 256),
            pl.ds(pl.multiple_of(head * 256, 256), 256),
        ]

    hx = []
    for k in range(1, NX):
        cols = pl.ds(pl.multiple_of(at_x(k) * 256, 256), 256)
        hx.append(
            go(send(hid.at[:, cols], h_at(x, h), hx_s.at[k - 1], hx_r.at[k - 1], dev_x(k)))
        )
    own_h = pltpu.make_async_copy(
        hid.at[:, pl.ds(pl.multiple_of(x * 256, 256), 256)], h_at(x, h), own_sem.at[6]
    )
    own_h.start()

    def w_step(n, s):
        pair = []
        for way in range(2):
            if s > 1:
                w_copies[(n, s - 1, way)].wait_recv()
        for way in range(2):
            back = (NZ - (s - 1)) if way == 0 else (s - 1)
            block = at_z(back) * 256
            if s < 4:
                rows = pl.ds(pl.multiple_of(block, 256), 256)
            else:
                rows = pl.ds(pl.multiple_of(block + 128 * way, 128), 128)
            ref = wg.at[n, rows]
            i = (n * 4 + s - 1) * 2 + way
            pair.append(go(send(ref, ref, w_s.at[i], w_r.at[i], dev_z(1 if way == 0 else NZ - 1))))
        w_copies[(n, s, 0)], w_copies[(n, s, 1)] = pair

    w_copies = {}

    lead = (0, 0, 1, 2, 3)

    def w_slot(t):
        for n in range(CHUNKS):
            s = t - lead[n]
            if 1 <= s <= 4:
                if s == 1:
                    own[n].wait()
                    if n == 4:
                        own[5].wait()
                w_step(n, s)

    def w_finish(n):
        for way in range(2):
            w_copies[(n, 4, way)].wait_recv()

    w_slot(1)

    def look_up(d, found):
        return jnp.where(ids[...] == d, place[d], found)

    found = lax.fori_loop(0, 512, look_up, jnp.zeros((32, 32), jnp.int32), unroll=8)
    placed[...] = found
    owner, local = found // 16, lax.rem(found, 16)
    order = lax.broadcasted_iota(jnp.int32, (32, 32), 1)
    line = lax.broadcasted_iota(jnp.int32, (32, 32), 0)
    spare = 32 * 16
    key = jnp.where(owner == r, order * 16 + local, spare)
    first = jnp.min(key, axis=1, keepdims=True)
    second_key = jnp.min(jnp.where(key > first, key, spare), axis=1, keepdims=True)
    choice = jnp.zeros((32, 1), jnp.int32)
    worst = jnp.zeros((32, 1), jnp.int32)
    for zo in range(NZ):
        doubled = jnp.zeros((32, 1), jnp.int32)
        pick = jnp.zeros((32, 1), jnp.int32)
        for xo in range(NX):
            held = jnp.sum((owner == zo * NX + xo).astype(jnp.int32), axis=1, keepdims=True)
            twice = (held > 1).astype(jnp.int32)
            doubled = doubled + twice
            pick = jnp.maximum(pick, twice * xo)
        worst = jnp.maximum(worst, doubled)
        choice = jnp.where(z == zo, pick, choice)
    worst = jnp.broadcast_to(jnp.max(worst, axis=0, keepdims=True), (32, 1))
    mine_row = placed[pl.ds(r, 1), :] // 16
    mine_wide = jnp.broadcast_to(mine_row, (32, 32))
    mine_col = jnp.sum(jnp.where(order == line, mine_wide, 0), axis=1, keepdims=True)
    later = jnp.max(
        ((mine_wide == mine_col) & (order < line)).astype(jnp.int32), axis=1, keepdims=True
    )
    slot = (mine_col // NX) * 5 + jnp.where(later > 0, 4, lax.rem(mine_col, NX))
    lane = lax.broadcasted_iota(jnp.int32, (32, 128), 1)
    table[...] = jnp.where(
        lane == 0,
        lax.rem(first, 16),
        jnp.where(lane == 1, lax.rem(second_key, 16), jnp.where(lane == 2, choice, jnp.where(lane == 3, slot, worst))),
    )
    to_scalars = pltpu.make_async_copy(table, tab, own_sem.at[11])
    to_scalars.start()
    to_scalars.wait()
    flag[0, 0] = tab[0, 4]
    for copy in docs_in:
        copy.wait()

    def pack(rank):
        def one(zt, carry):
            for k in range(NX):
                index = tab[zt * NX + at_x(k), rank]
                if k == 0:
                    here = xr1 if rank else xr
                    here[x, zt, 0] = dk[index]
                    here[x, zt, 1] = dv[index]
                else:
                    xs[k - 1, rank, zt, 0] = dk[index]
                    xs[k - 1, rank, zt, 1] = dv[index]
            return carry

        lax.fori_loop(0, NZ, one, 0)

    def send_docs_x(rank):
        there = (xr1 if rank else xr).at[x]
        copies = []
        for k in range(1, NX):
            i = rank * 3 + k - 1
            copies.append(
                go(send(xs.at[k - 1, rank], there, dx_s.at[i], dx_r.at[i], dev_x(k)))
            )
        return copies

    pack(0)
    docs_x = send_docs_x(0)
    w_slot(2)
    pack(1)
    for copy in hx:
        copy.wait_recv()
    own_h.wait()

    def h_cols(head, rows=slice(0, 1024)):
        return hg.at[
            pl.ds(rows.start, rows.stop - rows.start), pl.ds(pl.multiple_of(head * 256, 256), 256)
        ]

    hy, hs = [], []
    for way, k in ((0, 1), (1, 3)):
        hy.append(go(send(h_cols(h), h_cols(h), hy_s.at[way], hy_r.at[way], dev_y(k))))
    hs.append(go(send(h_cols(h), h_cols(h), hs_s.at[0], hs_r.at[0], sibling)))
    w_slot(3)
    mask()
    w_slot(4)
    docs_x1 = send_docs_x(1)
    for copy in hy:
        copy.wait_recv()
    top, bottom = slice(0, 512), slice(512, 1024)
    left, right = head_y(3), head_y(1)
    hy2 = [
        go(send(h_cols(left, top), h_cols(left, top), hy_s.at[2], hy_r.at[2], dev_y(1))),
        go(send(h_cols(right, bottom), h_cols(right, bottom), hy_s.at[3], hy_r.at[3], dev_y(3))),
    ]
    hs.append(go(send(h_cols(left), h_cols(left), hs_s.at[1], hs_r.at[1], sibling)))
    hs.append(go(send(h_cols(right), h_cols(right), hs_s.at[2], hs_r.at[2], sibling)))
    w_slot(5)
    for copy in hy2:
        copy.wait_recv()
    far = head_y(2)
    hs.append(go(send(h_cols(far), h_cols(far), hs_s.at[3], hs_r.at[3], sibling)))
    for copy in hs:
        copy.wait_recv()

    def product(n, k):
        block = lax.rem(x + k, NX)
        rows = pl.ds(pl.multiple_of(block * 256, 256), 256)
        part[n, block] = jnp.dot(hg[rows, :], wg[n], preferred_element_type=jnp.float32)

    r1_copies, r2_copies = {}, {}

    def multiply(n):
        w_finish(n)
        product(n, 2)
        far_x = at_x(2)
        r1_copies[n] = [
            go(
                send(
                    part.at[n, far_x, pl.ds(128 * way, 128)],
                    r1.at[n, way],
                    r1_s.at[n * 2 + way],
                    r1_r.at[n * 2 + way],
                    dev_x(1 if way == 0 else 3),
                )
            )
            for way in range(2)
        ]

        def rest(k, carry):
            product(n, k)
            return carry

        lax.fori_loop(3, 6, rest, 0)

    def second(n):
        for copy in r1_copies[n]:
            copy.wait_recv()
        part[n, at_x(1), pl.ds(0, 128)] = part[n, at_x(1), pl.ds(0, 128)] + r1[n, 0]
        part[n, at_x(3), pl.ds(128, 128)] = part[n, at_x(3), pl.ds(128, 128)] + r1[n, 1]
        r2_copies[n] = [
            go(
                send(
                    part.at[n, at_x(1 if way == 0 else 3)],
                    r2.at[n, way],
                    r2_s.at[n * 2 + way],
                    r2_r.at[n * 2 + way],
                    dev_x(1 if way == 0 else 3),
                )
            )
            for way in range(2)
        ]

    def third(n):
        for copy in r2_copies[n]:
            copy.wait_recv()
        total = (part[n, x] + r2[n, 0] + r2[n, 1]).astype(jnp.bfloat16)
        if n < 4:
            for i in range(2):
                for g in range(2):
                    q_out[pl.ds(i * 1024 + (2 * n + g) * 128, 128)] = total[
                        i * 128 : (i + 1) * 128, g * HD : (g + 1) * HD
                    ]
        else:
            nk_out[...] = total[:, :HD]
            nv_out[...] = total[:, HD:]

    w_slot(6)
    multiply(0)
    w_slot(7)
    for copy in docs_x:
        copy.wait_recv()
    docs_z = []
    for k in (4, 3, 5, 2, 6, 1, 7):
        docs_z.append(
            go(
                send(
                    xr.at[:, at_z(k)],
                    zr.at[z, pl.ds(0, 4)],
                    dz_s.at[k - 1],
                    dz_r.at[k - 1],
                    dev_z(k),
                )
            )
        )
    own_z = pltpu.make_async_copy(xr.at[:, z], zr.at[z, pl.ds(0, 4)], own_sem.at[7])
    own_z.start()

    multiply(1)
    multiply(2)
    second(0)
    multiply(3)
    second(1)
    multiply(4)
    for copy in docs_x1:
        copy.wait_recv()

    def extra(zt, carry):
        chosen = tab[zt * NX + x, 2]
        ex[zt] = xr1[chosen, zt]
        return carry

    lax.fori_loop(0, NZ, extra, 0)
    docs_e = []
    for k in (4, 3, 5, 2, 6, 1, 7):
        docs_e.append(
            go(send(ex.at[at_z(k)], zr.at[z, 4], de_s.at[k - 1], de_r.at[k - 1], dev_z(k)))
        )
    own_e = pltpu.make_async_copy(ex.at[z], zr.at[z, 4], own_sem.at[8])
    own_e.start()


    second(2)
    third(0)
    second(3)
    third(1)
    second(4)
    third(2)
    third(3)
    third(4)
    own_z.wait()
    own_e.wait()
    for copy in docs_z:
        copy.wait_recv()
    for copy in docs_e:
        copy.wait_recv()
    span = SLOTS * BLK
    for i in range(2):

        def fetch(j, carry):
            slot = tab[i * NDOC + j, 3]
            at = pl.ds(pl.multiple_of(j * span, span), span)
            keys[i, at] = zr[slot // 5, lax.rem(slot, 5), 0]
            values[i, at] = zr[slot // 5, lax.rem(slot, 5), 1]
            return carry

        lax.fori_loop(0, NDOC, fetch, 0)
        keys[i, pl.ds(NDOC * span, 128)] = nk_out[pl.ds(i * 128, 128)]
        values[i, pl.ds(NDOC * span, 128)] = nv_out[pl.ds(i * 128, 128)]

    factor = math.log2(math.e) / math.sqrt(HD)

    def score(step, side):
        i = step // 4
        at = pl.ds(pl.multiple_of(step * 256, 256), 256)
        scores = lax.dot_general(
            q_out[at], keys[i], (((1,), (1,)), ((), ())), preferred_element_type=jnp.float32
        )
        scores = scores * factor + bias[i]
        points[side] = scores
        peaks[side] = jnp.broadcast_to(jnp.max(scores, axis=-1, keepdims=True), (256, 128))

    def weigh(step, side):
        i, p = step // 4, lax.rem(step, 4)
        weights = jnp.exp2(points[side] - peaks[side][:, :1])
        share = 1.0 / jnp.sum(weights, axis=-1, keepdims=True)
        probs = (weights * share).astype(jnp.bfloat16)
        result = jnp.dot(probs, values[i], preferred_element_type=jnp.float32).astype(jnp.bfloat16)
        at = pl.ds(pl.multiple_of(i * 128, 128), 128)
        for g in range(2):
            cols = pl.ds(pl.multiple_of(p * 256 + g * HD, HD), HD)
            out[at, cols] = result[g * 128 : (g + 1) * 128]

    score(0, 0)

    def attend_two(k, carry):
        score(2 * k + 1, 1)
        weigh(2 * k, 0)
        score(lax.rem(2 * k + 2, 8), 0)
        weigh(2 * k + 1, 1)
        return carry

    lax.fori_loop(0, 4, attend_two, 0)
    for copy in started:
        copy.wait_send()


def fused(rows, place, ids, kept, counts, hid, dk, dv, wq, wk, wv):
    vmem = pl.BlockSpec(memory_space=pltpu.VMEM)
    smem = pl.BlockSpec(memory_space=pltpu.SMEM)
    anym = pl.BlockSpec(memory_space=pl.ANY)
    dma = pltpu.SemaphoreType.DMA
    bf16, f32 = jnp.bfloat16, jnp.float32
    context = NDOC * SLOTS * BLK + 128
    return pl.pallas_call(
        exchange_kernel,
        out_shape=(
            jax.ShapeDtypeStruct((256, 1024), bf16),
            jax.ShapeDtypeStruct((2048, HD), bf16),
            jax.ShapeDtypeStruct((256, HD), bf16),
            jax.ShapeDtypeStruct((256, HD), bf16),
            jax.ShapeDtypeStruct((1, 1), jnp.int32),
        ),
        in_specs=[smem, smem, vmem, vmem, vmem, anym, anym, anym, anym, anym, anym],
        out_specs=(vmem, vmem, vmem, vmem, smem),
        scratch_shapes=[
            pltpu.VMEM((32, 32), jnp.int32),
            pltpu.VMEM((32, 128), jnp.int32),
            pltpu.SMEM((32, 128), jnp.int32),
            pltpu.VMEM((16, 128, HD), bf16),
            pltpu.VMEM((16, 128, HD), bf16),
            pltpu.VMEM((2, context, HD), bf16),
            pltpu.VMEM((2, context, HD), bf16),
            pltpu.VMEM((2, 1, context), f32),
            pltpu.VMEM((2, 256, context), f32),
            pltpu.VMEM((2, 256, 128), f32),
            pltpu.VMEM((1024, 2048), bf16),
            pltpu.VMEM((CHUNKS, 2048, COLS), bf16),
            pltpu.VMEM((CHUNKS, NX, 256, COLS), f32),
            pltpu.VMEM((CHUNKS, 2, 128, COLS), f32),
            pltpu.VMEM((CHUNKS, 2, 256, COLS), f32),
            pltpu.VMEM((3, 2, NZ, 2, 128, HD), bf16),
            pltpu.VMEM((NX, NZ, 2, 128, HD), bf16),
            pltpu.VMEM((NX, NZ, 2, 128, HD), bf16),
            pltpu.VMEM((NZ, 2, 128, HD), bf16),
            pltpu.VMEM((NZ, 5, 2, 128, HD), bf16),
            dma((12,)),
            dma((3,)),
            dma((3,)),
            dma((4,)),
            dma((4,)),
            dma((4,)),
            dma((4,)),
            dma((40,)),
            dma((40,)),
            dma((10,)),
            dma((10,)),
            dma((10,)),
            dma((10,)),
            dma((6,)),
            dma((6,)),
            dma((7,)),
            dma((7,)),
            dma((7,)),
            dma((7,)),
        ],
        compiler_params=pltpu.CompilerParams(
            collective_id=0, has_side_effects=True, vmem_limit_bytes=60 * 2**20
        ),
    )(rows, place, ids, kept, counts, hid, dk, dv, wq, wk, wv)


def shards(
    hidden,
    w_query,
    w_key,
    w_value,
    doc_keys,
    doc_values,
    slot_counts,
    kept_blocks,
    doc_ids,
    doc_place,
    recompute_rows,
):
    owners = lax.axis_size("req")
    refs = 2 * NDOC
    ids = doc_ids.reshape(owners, refs)
    attended, queries, keys_new, values_new, flag = fused(
        recompute_rows,
        doc_place,
        ids,
        kept_blocks.reshape(512, SLOTS).T,
        slot_counts.T,
        hidden.reshape(256, -1),
        doc_keys.reshape(16, 128, HD),
        doc_values.reshape(16, 128, HD),
        w_query,
        w_key,
        w_value,
    )

    def again():
        return general(
            queries.reshape(2, 8, 128, HD).transpose(0, 2, 1, 3).reshape(256, 1024),
            keys_new,
            values_new,
            doc_keys,
            doc_values,
            slot_counts,
            kept_blocks,
            doc_ids,
            doc_place,
            recompute_rows,
        ).reshape(256, 1024)

    attended = lax.cond(flag[0, 0] > 1, again, lambda: attended)
    return (
        attended.reshape(2, 128, 1024),
        keys_new.reshape(2, 128, HD),
        values_new.reshape(2, 128, HD),
    )


def solution(mesh):
    return jax.shard_map(
        shards,
        mesh=mesh,
        in_specs=(
            P("req", None, "head"),
            P("req", "head"),
            P("req", "head"),
            P("req", "head"),
            P("req", "head", None, None),
            P("req", "head", None, None),
            P(None, "head"),
            P(None, "head", None),
            P(),
            P(),
            P("req", None),
        ),
        out_specs=(P("req", None, "head"), P("req", None, "head"), P("req", None, "head")),
        check_vma=False,
    )
```

time: 183 us -> 136 us (0.74); the launches traced: 181 us -> 136 us
  Pallas kernels: 155 us -> 129 us
  between operations: 14.7 us -> 1.39 us
  other arithmetic: 2.99 us -> 0 us
  local copies, waits for them, and re-layouts: 7.27 us -> 4.72 us
    pallas_call x2 -> x1, Pallas kernels: 155 us -> 129 us  [fused(): pl.pallas_call(exchange_kernel, out_shape=(jax.ShapeDtypeStruct((256, 102...]
    unnamed x3 -> x18, local copies, waits for them, and re-layouts: 2.04 us -> 4.04 us
    another operation x4 -> x0, local copies, waits for them, and re-layouts: 1.84 us -> none
    cond x4 -> x0, local copies, waits for them, and re-layouts: 1.83 us -> none
where the time goes in v2:
time: 136 us
  Pallas kernels  129 us (95%)
  local copies, waits for them, and re-layouts  4.72 us (3%)
  between operations  1.39 us (1%)
    pallas_call x1, Pallas kernels, fused(): pl.pallas_call(exchange_kernel, out_shape=(jax.ShapeDtypeStruct((256, 102...  129 us
    unnamed x18, local copies, waits for them, and re-layouts  4.04 us

profile of v2, /device:TPU:1, one launch (start us, length us, event | category | flops | bytes accessed | tf_op | source)
XLA Modules:
  0.0 135.7 jit_solution(7346180265499092775)
XLA Ops:
  0.6 0.0 copy-start.8
  0.6 0.0 copy-start
  0.7 0.0 copy-start.7
  0.7 0.0 copy-start.6
  0.7 0.0 copy-start.1
  0.7 0.0 copy-start.3
  0.7 0.0 copy-start.2
  0.7 0.9 copy.62
  1.6 0.7 reshape.449.ids
  2.3 129.3 %shard_map.130 = (bf16[256,1024]{1,0:T(8,128)(2,1)}, bf16[2048,128]{1,0:T(8,128)(2,1)}, bf16[256,128]{1,0:T(8,128)(2,1)S(1)}, bf16[256,128]{1,0:T(8,128)(2,1)S(1)}, s32[1,1]{1,0:T(1,128)}) custom-call(s32[2,128]{1,0:T(2,128)} %rows.1, s32[512]{0:T(512)} %place.1, s32[32,32]{1,0:T(8,128)} %reshape.449.ids, s32[8,512]{1,0:T(8,128)} %bitcast.140, ...), custom_call_target="tpu_custom_call" | custom-call | tf_op jit(solution)/shard_map/pallas_call | solution.py:640
  132.2 0.0 copy-done.8
  132.2 0.0 copy-done
  132.3 0.0 copy-done.7
  132.3 0.0 copy-done.6
  132.3 0.0 copy-done.1
  132.3 0.0 copy-done.3
  132.3 0.0 copy-done.2
  132.3 0.2 conditional.1
  132.5 1.9 %copy.78 = bf16[2,128,1024]{2,1,0:T(8,128)(2,1)} copy(bf16[2,128,1024]{2,1,0:T(8,128)(2,1)} %get-tuple-element.183) | data formatting | bytes 1048576
  134.4 0.6 copy.79
  135.0 0.6 copy.80
Async XLA Ops:
  0.6 131.6 %copy-start.8 = (s32[2,128]{1,0:T(2,128)S(1)}, s32[2,128]{1,0:T(2,128)}, u32[]{:S(2)}) copy-start(s32[2,128]{1,0:T(2,128)} %rows.1) | copy-start | bytes 3076
  0.6 131.6 %copy-start = (s32[512]{0:T(512)S(1)}, s32[512]{0:T(512)}, u32[]{:S(2)}) copy-start(s32[512]{0:T(512)} %place.1) | copy-start | bytes 6148
  0.7 131.6 %copy-start.7 = (s32[64,16]{0,1:T(8,128)S(1)}, s32[64,16]{0,1:T(8,128)}, u32[]{:S(2)}) copy-start(s32[64,16]{0,1:T(8,128)} %param.21) | copy-start | bytes 12292
  0.7 131.6 %copy-start.6 = (s32[512,1,8]{0,2,1:T(8,128)S(1)}, s32[512,1,8]{0,2,1:T(8,128)}, u32[]{:S(2)}) copy-start(s32[512,1,8]{0,2,1:T(8,128)} %param.20) | copy-start | bytes 49156
  0.7 131.6 %copy-start.1 = (s32[512,1]{0,1:T(1,128)S(1)}, s32[512,1]{0,1:T(1,128)}, u32[]{:S(2)}) copy-start(s32[512,1]{0,1:T(1,128)} %param.19) | copy-start | bytes 6148
  0.7 131.6 %copy-start.3 = (bf16[16,1,128,128]{3,2,1,0:T(8,128)(2,1)S(1)}, bf16[16,1,128,128]{3,2,1,0:T(8,128)(2,1)}, u32[]{:S(2)}) copy-start(bf16[16,1,128,128]{3,2,1,0:T(8,128)(2,1)} %param.18) | copy-start | bytes 1572868
  0.7 131.6 %copy-start.2 = (bf16[16,1,128,128]{3,2,1,0:T(8,128)(2,1)S(1)}, bf16[16,1,128,128]{3,2,1,0:T(8,128)(2,1)}, u32[]{:S(2)}) copy-start(bf16[16,1,128,128]{3,2,1,0:T(8,128)(2,1)} %param.17) | copy-start | bytes 1572868

commit v3 on v2

--- a/solution.py
+++ b/solution.py
@@ -150,7 +150,7 @@
     values,
     bias,
     points,
-    peaks,
+    shares,
     hg,
     wg,
     part,
@@ -160,7 +160,9 @@
     xr,
     xr1,
     ex,
-    zr,
+    inbox,
+    zk,
+    zv,
     own_sem,
     hx_s,
     hx_r,
@@ -216,18 +218,20 @@
         pltpu.make_async_copy(dv_in, dv, own_sem.at[10]),
     ]
     own = []
+    own.append(
+        pltpu.make_async_copy(wk, wg.at[0, pl.ds(z * 256, 256), pl.ds(0, HD)], own_sem.at[0])
+    )
+    own.append(
+        pltpu.make_async_copy(wv, wg.at[0, pl.ds(z * 256, 256), pl.ds(HD, HD)], own_sem.at[5])
+    )
     for n in range(4):
         own.append(
             pltpu.make_async_copy(
-                wq.at[:, pl.ds(n * COLS, COLS)], wg.at[n, pl.ds(z * 256, 256)], own_sem.at[n]
+                wq.at[:, pl.ds(n * COLS, COLS)],
+                wg.at[n + 1, pl.ds(z * 256, 256)],
+                own_sem.at[n + 1],
             )
         )
-    own.append(
-        pltpu.make_async_copy(wk, wg.at[4, pl.ds(z * 256, 256), pl.ds(0, HD)], own_sem.at[4])
-    )
-    own.append(
-        pltpu.make_async_copy(wv, wg.at[4, pl.ds(z * 256, 256), pl.ds(HD, HD)], own_sem.at[5])
-    )
     for copy in own + docs_in:
         copy.start()
 
@@ -338,9 +342,9 @@
             s = t - lead[n]
             if 1 <= s <= 4:
                 if s == 1:
-                    own[n].wait()
-                    if n == 4:
-                        own[5].wait()
+                    own[n + 1].wait()
+                    if n == 0:
+                        own[0].wait()
                 w_step(n, s)
 
     def w_finish(n):
@@ -362,7 +366,11 @@
     first = jnp.min(key, axis=1, keepdims=True)
     second_key = jnp.min(jnp.where(key > first, key, spare), axis=1, keepdims=True)
     choice = jnp.zeros((32, 1), jnp.int32)
+    spares = jnp.zeros((32, 1), jnp.int32)
     worst = jnp.zeros((32, 1), jnp.int32)
+    above = jnp.zeros((32, 1), jnp.int32)
+    below = jnp.zeros((32, 1), jnp.int32)
+    target_z = lax.broadcasted_iota(jnp.int32, (32, 1), 0) // NX
     for zo in range(NZ):
         doubled = jnp.zeros((32, 1), jnp.int32)
         pick = jnp.zeros((32, 1), jnp.int32)
@@ -372,7 +380,12 @@
             doubled = doubled + twice
             pick = jnp.maximum(pick, twice * xo)
         worst = jnp.maximum(worst, doubled)
+        away = lax.rem(zo - target_z + NZ, NZ)
+        above = above + jnp.where((away >= 1) & (away <= 4), doubled, 0)
+        below = below + jnp.where(away >= 5, doubled, 0)
         choice = jnp.where(z == zo, pick, choice)
+        spares = jnp.where(z == zo, doubled, spares)
+    worst = jnp.maximum(worst, jnp.maximum(above, below))
     worst = jnp.broadcast_to(jnp.max(worst, axis=0, keepdims=True), (32, 1))
     mine_row = placed[pl.ds(r, 1), :] // 16
     mine_wide = jnp.broadcast_to(mine_row, (32, 32))
@@ -380,12 +393,14 @@
     later = jnp.max(
         ((mine_wide == mine_col) & (order < line)).astype(jnp.int32), axis=1, keepdims=True
     )
-    slot = (mine_col // NX) * 5 + jnp.where(later > 0, 4, lax.rem(mine_col, NX))
+    away = lax.rem(mine_col // NX - z + NZ, NZ)
+    spare_slot = jnp.where(away == 0, 32, jnp.where(away <= 4, 33, 34))
+    slot = jnp.where(later > 0, spare_slot, mine_col)
     lane = lax.broadcasted_iota(jnp.int32, (32, 128), 1)
     table[...] = jnp.where(
         lane == 0,
         lax.rem(first, 16),
-        jnp.where(lane == 1, lax.rem(second_key, 16), jnp.where(lane == 2, choice, jnp.where(lane == 3, slot, worst))),
+        jnp.where(lane == 1, lax.rem(second_key, 16), jnp.where(lane == 2, choice, jnp.where(lane == 3, slot, jnp.where(lane == 4, worst, spares)))),
     )
     to_scalars = pltpu.make_async_copy(table, tab, own_sem.at[11])
     to_scalars.start()
@@ -419,10 +434,11 @@
             )
         return copies
 
+    pack(1)
+    docs_x1 = send_docs_x(1)
+    w_slot(2)
     pack(0)
     docs_x = send_docs_x(0)
-    w_slot(2)
-    pack(1)
     for copy in hx:
         copy.wait_recv()
     own_h.wait()
@@ -439,7 +455,6 @@
     w_slot(3)
     mask()
     w_slot(4)
-    docs_x1 = send_docs_x(1)
     for copy in hy:
         copy.wait_recv()
     top, bottom = slice(0, 512), slice(512, 1024)
@@ -510,36 +525,150 @@
         for copy in r2_copies[n]:
             copy.wait_recv()
         total = (part[n, x] + r2[n, 0] + r2[n, 1]).astype(jnp.bfloat16)
-        if n < 4:
+        if n > 0:
             for i in range(2):
                 for g in range(2):
-                    q_out[pl.ds(i * 1024 + (2 * n + g) * 128, 128)] = total[
+                    q_out[pl.ds(i * 1024 + (2 * n - 2 + g) * 128, 128)] = total[
                         i * 128 : (i + 1) * 128, g * HD : (g + 1) * HD
                     ]
         else:
             nk_out[...] = total[:, :HD]
             nv_out[...] = total[:, HD:]
 
+    for copy in docs_x1:
+        copy.wait_recv()
+
+    def extra(zt, carry):
+        chosen = tab[zt * NX + x, 2]
+        ex[zt] = xr1[chosen, zt]
+        return carry
+
+    lax.fori_loop(0, NZ, extra, 0)
+    own_e = [
+        pltpu.make_async_copy(ex.at[z, kv], held.at[32], own_sem.at[8 + 4 * kv])
+        for kv, held in ((0, zk), (1, zv))
+    ]
+    for copy in own_e:
+        copy.start()
+
+    spare_copies = {}
+
+    def spare_step(s):
+        for way, (step, reach) in enumerate(((NZ - 1, 4), (1, 3))):
+            if s > reach:
+                continue
+            left_to_go = reach + 1 - s
+            target = at_z(NZ - left_to_go if way == 0 else left_to_go)
+            if s > 1:
+                spare_copies[(s - 1, way)].wait_recv()
+                mine = tab[target * NX + x, 5] > 0
+                ex[target] = jnp.where(mine, ex[target], inbox[way * 3 + s - 2])
+            i = way * 4 + s - 1
+            if s < reach:
+                there = inbox.at[way * 3 + s - 1]
+                spare_copies[(s, way)] = go(
+                    send(ex.at[target], there, de_s.at[i], de_r.at[i], dev_z(step))
+                )
+            else:
+                for kv, held in ((0, zk), (1, zv)):
+                    j = i if kv == 0 else 8 + way
+                    spare_copies[("end", way, kv)] = go(
+                        send(
+                            ex.at[target, kv],
+                            held.at[33 + way],
+                            de_s.at[j],
+                            de_r.at[j],
+                            dev_z(step),
+                        )
+                    )
+
+    spare_step(1)
     w_slot(6)
+    spare_step(2)
     multiply(0)
     w_slot(7)
+    spare_step(3)
+    spare_step(4)
     for copy in docs_x:
         copy.wait_recv()
-    docs_z = []
-    for k in (4, 3, 5, 2, 6, 1, 7):
-        docs_z.append(
-            go(
-                send(
-                    xr.at[:, at_z(k)],
-                    zr.at[z, pl.ds(0, 4)],
-                    dz_s.at[k - 1],
-                    dz_r.at[k - 1],
-                    dev_z(k),
+    docs_z, own_z = ([], []), []
+    for kv, held in ((0, zk), (1, zv)):
+        for k in (4, 3, 5, 2, 6, 1, 7):
+            i = kv * 7 + k - 1
+            docs_z[kv].append(
+                go(
+                    send(
+                        xr.at[:, at_z(k), kv],
+                        held.at[pl.ds(z * NX, NX)],
+                        dz_s.at[i],
+                        dz_r.at[i],
+                        dev_z(k),
+                    )
                 )
             )
-        )
-    own_z = pltpu.make_async_copy(xr.at[:, z], zr.at[z, pl.ds(0, 4)], own_sem.at[7])
-    own_z.start()
+        own_z.append(
+            pltpu.make_async_copy(
+                xr.at[:, z, kv], held.at[pl.ds(z * NX, NX)], own_sem.at[7 if kv == 0 else 13]
+            )
+        )
+        own_z[kv].start()
+
+    def arrived(kv):
+        own_z[kv].wait()
+        own_e[kv].wait()
+        for copy in docs_z[kv]:
+            copy.wait_recv()
+        for way in range(2):
+            spare_copies[("end", way, kv)].wait_recv()
+
+    span = SLOTS * BLK
+    factor = math.log2(math.e) / math.sqrt(HD)
+
+    def fetch(kv, held, context, fresh):
+        arrived(kv)
+        for i in range(2):
+
+            def one(j, carry):
+                at = pl.ds(pl.multiple_of(j * span, span), span)
+                context[i, at] = held[tab[i * NDOC + j, 3]]
+                return carry
+
+            lax.fori_loop(0, NDOC, one, 0)
+            context[i, pl.ds(NDOC * span, 128)] = fresh[pl.ds(i * 128, 128)]
+
+    def score(i, p):
+        step = i * 4 + p
+        scores = lax.dot_general(
+            q_out[pl.ds(step * 256, 256)],
+            keys[i],
+            (((1,), (1,)), ((), ())),
+            preferred_element_type=jnp.float32,
+        )
+        scores = scores * factor + bias[i]
+        points[step] = scores
+        return jnp.max(scores, axis=-1, keepdims=True)
+
+    def spread_out(i, p, peak):
+        step = i * 4 + p
+        weights = jnp.exp2(points[step] - peak)
+        points[step] = weights
+        share = 1.0 / jnp.sum(weights, axis=-1, keepdims=True)
+        shares[step] = jnp.broadcast_to(share, (256, 128))
+
+    def heads(p):
+        peaks = [score(i, p) for i in range(2)]
+        for i in range(2):
+            spread_out(i, p, peaks[i])
+
+    def gather_values(step, carry):
+        i, p = step // 4, lax.rem(step, 4)
+        probs = (points[step] * shares[step][:, :1]).astype(jnp.bfloat16)
+        result = jnp.dot(probs, values[i], preferred_element_type=jnp.float32).astype(jnp.bfloat16)
+        at = pl.ds(pl.multiple_of(i * 128, 128), 128)
+        for g in range(2):
+            cols = pl.ds(pl.multiple_of(p * 256 + g * HD, HD), HD)
+            out[at, cols] = result[g * 128 : (g + 1) * 128]
+        return carry
 
     multiply(1)
     multiply(2)
@@ -547,85 +676,16 @@
     multiply(3)
     second(1)
     multiply(4)
-    for copy in docs_x1:
-        copy.wait_recv()
-
-    def extra(zt, carry):
-        chosen = tab[zt * NX + x, 2]
-        ex[zt] = xr1[chosen, zt]
-        return carry
-
-    lax.fori_loop(0, NZ, extra, 0)
-    docs_e = []
-    for k in (4, 3, 5, 2, 6, 1, 7):
-        docs_e.append(
-            go(send(ex.at[at_z(k)], zr.at[z, 4], de_s.at[k - 1], de_r.at[k - 1], dev_z(k)))
-        )
-    own_e = pltpu.make_async_copy(ex.at[z], zr.at[z, 4], own_sem.at[8])
-    own_e.start()
-
-
     second(2)
+    second(3)
+    second(4)
     third(0)
-    second(3)
-    third(1)
-    second(4)
-    third(2)
-    third(3)
-    third(4)
-    own_z.wait()
-    own_e.wait()
-    for copy in docs_z:
-        copy.wait_recv()
-    for copy in docs_e:
-        copy.wait_recv()
-    span = SLOTS * BLK
-    for i in range(2):
-
-        def fetch(j, carry):
-            slot = tab[i * NDOC + j, 3]
-            at = pl.ds(pl.multiple_of(j * span, span), span)
-            keys[i, at] = zr[slot // 5, lax.rem(slot, 5), 0]
-            values[i, at] = zr[slot // 5, lax.rem(slot, 5), 1]
-            return carry
-
-        lax.fori_loop(0, NDOC, fetch, 0)
-        keys[i, pl.ds(NDOC * span, 128)] = nk_out[pl.ds(i * 128, 128)]
-        values[i, pl.ds(NDOC * span, 128)] = nv_out[pl.ds(i * 128, 128)]
-
-    factor = math.log2(math.e) / math.sqrt(HD)
-
-    def score(step, side):
-        i = step // 4
-        at = pl.ds(pl.multiple_of(step * 256, 256), 256)
-        scores = lax.dot_general(
-            q_out[at], keys[i], (((1,), (1,)), ((), ())), preferred_element_type=jnp.float32
-        )
-        scores = scores * factor + bias[i]
-        points[side] = scores
-        peaks[side] = jnp.broadcast_to(jnp.max(scores, axis=-1, keepdims=True), (256, 128))
-
-    def weigh(step, side):
-        i, p = step // 4, lax.rem(step, 4)
-        weights = jnp.exp2(points[side] - peaks[side][:, :1])
-        share = 1.0 / jnp.sum(weights, axis=-1, keepdims=True)
-        probs = (weights * share).astype(jnp.bfloat16)
-        result = jnp.dot(probs, values[i], preferred_element_type=jnp.float32).astype(jnp.bfloat16)
-        at = pl.ds(pl.multiple_of(i * 128, 128), 128)
-        for g in range(2):
-            cols = pl.ds(pl.multiple_of(p * 256 + g * HD, HD), HD)
-            out[at, cols] = result[g * 128 : (g + 1) * 128]
-
-    score(0, 0)
-
-    def attend_two(k, carry):
-        score(2 * k + 1, 1)
-        weigh(2 * k, 0)
-        score(lax.rem(2 * k + 2, 8), 0)
-        weigh(2 * k + 1, 1)
-        return carry
-
-    lax.fori_loop(0, 4, attend_two, 0)
+    fetch(0, zk, keys, nk_out)
+    for n in range(1, CHUNKS):
+        third(n)
+        heads(n - 1)
+    fetch(1, zv, values, nv_out)
+    lax.fori_loop(0, 8, gather_values, 0)
     for copy in started:
         copy.wait_send()
 
@@ -657,8 +717,8 @@
             pltpu.VMEM((2, context, HD), bf16),
             pltpu.VMEM((2, context, HD), bf16),
             pltpu.VMEM((2, 1, context), f32),
-            pltpu.VMEM((2, 256, context), f32),
-            pltpu.VMEM((2, 256, 128), f32),
+            pltpu.VMEM((8, 256, context), f32),
+            pltpu.VMEM((8, 256, 128), f32),
             pltpu.VMEM((1024, 2048), bf16),
             pltpu.VMEM((CHUNKS, 2048, COLS), bf16),
             pltpu.VMEM((CHUNKS, NX, 256, COLS), f32),
@@ -668,8 +728,10 @@
             pltpu.VMEM((NX, NZ, 2, 128, HD), bf16),
             pltpu.VMEM((NX, NZ, 2, 128, HD), bf16),
             pltpu.VMEM((NZ, 2, 128, HD), bf16),
-            pltpu.VMEM((NZ, 5, 2, 128, HD), bf16),
-            dma((12,)),
+            pltpu.VMEM((5, 2, 128, HD), bf16),
+            pltpu.VMEM((35, 128, HD), bf16),
+            pltpu.VMEM((35, 128, HD), bf16),
+            dma((14,)),
             dma((3,)),
             dma((3,)),
             dma((4,)),
@@ -684,10 +746,10 @@
             dma((10,)),
             dma((6,)),
             dma((6,)),
-            dma((7,)),
-            dma((7,)),
-            dma((7,)),
-            dma((7,)),
+            dma((14,)),
+            dma((14,)),
+            dma((10,)),
+            dma((10,)),
         ],
         compiler_params=pltpu.CompilerParams(
             collective_id=0, has_side_effects=True, vmem_limit_bytes=60 * 2**20

time: 136 us -> 127 us (0.934); the launches traced: 136 us -> 124 us
  Pallas kernels: 129 us -> 118 us
    pallas_call x1, Pallas kernels: 129 us -> 118 us  [fused(): pl.pallas_call(exchange_kernel, out_shape=(jax.ShapeDtypeStruct((256, 102...]
where the time goes in v3:
time: 127 us; the launch traced here: 124 us
  Pallas kernels  118 us (93%)
  local copies, waits for them, and re-layouts  4.72 us (4%)
  between operations  1.39 us (1%)
    pallas_call x1, Pallas kernels, fused(): pl.pallas_call(exchange_kernel, out_shape=(jax.ShapeDtypeStruct((256, 102...  118 us
    unnamed x18, local copies, waits for them, and re-layouts  4.04 us

profile of v3, /device:TPU:1, one launch (start us, length us, event | category | flops | bytes accessed | tf_op | source)
XLA Modules:
  0.0 124.3 jit_solution(4748412096610002663)
XLA Ops:
  0.6 0.0 copy-start.8
  0.6 0.0 copy-start
  0.7 0.0 copy-start.7
  0.7 0.0 copy-start.6
  0.7 0.0 copy-start.1
  0.7 0.0 copy-start.3
  0.7 0.0 copy-start.2
  0.7 0.9 copy.62
  1.6 0.7 reshape.449.ids
  2.3 118.0 %shard_map.130 = (bf16[256,1024]{1,0:T(8,128)(2,1)}, bf16[2048,128]{1,0:T(8,128)(2,1)}, bf16[256,128]{1,0:T(8,128)(2,1)S(1)}, bf16[256,128]{1,0:T(8,128)(2,1)S(1)}, s32[1,1]{1,0:T(1,128)}) custom-call(s32[2,128]{1,0:T(2,128)} %rows.1, s32[512]{0:T(512)} %place.1, s32[32,32]{1,0:T(8,128)} %reshape.449.ids, s32[8,512]{1,0:T(8,128)} %bitcast.140, ...), custom_call_target="tpu_custom_call" | custom-call | tf_op jit(solution)/shard_map/pallas_call | solution.py:700
  120.9 0.0 copy-done.8
  120.9 0.0 copy-done
  120.9 0.0 copy-done.7
  120.9 0.0 copy-done.6
  120.9 0.0 copy-done.1
  120.9 0.0 copy-done.3
  120.9 0.0 copy-done.2
  120.9 0.2 conditional.1
  121.2 1.9 %copy.78 = bf16[2,128,1024]{2,1,0:T(8,128)(2,1)} copy(bf16[2,128,1024]{2,1,0:T(8,128)(2,1)} %get-tuple-element.183) | data formatting | bytes 1048576
  123.0 0.6 copy.79
  123.7 0.6 copy.80
Async XLA Ops:
  0.6 120.2 %copy-start.8 = (s32[2,128]{1,0:T(2,128)S(1)}, s32[2,128]{1,0:T(2,128)}, u32[]{:S(2)}) copy-start(s32[2,128]{1,0:T(2,128)} %rows.1) | copy-start | bytes 3076
  0.6 120.2 %copy-start = (s32[512]{0:T(512)S(1)}, s32[512]{0:T(512)}, u32[]{:S(2)}) copy-start(s32[512]{0:T(512)} %place.1) | copy-start | bytes 6148
  0.7 120.2 %copy-start.7 = (s32[64,16]{0,1:T(8,128)S(1)}, s32[64,16]{0,1:T(8,128)}, u32[]{:S(2)}) copy-start(s32[64,16]{0,1:T(8,128)} %param.21) | copy-start | bytes 12292
  0.7 120.2 %copy-start.6 = (s32[512,1,8]{0,2,1:T(8,128)S(1)}, s32[512,1,8]{0,2,1:T(8,128)}, u32[]{:S(2)}) copy-start(s32[512,1,8]{0,2,1:T(8,128)} %param.20) | copy-start | bytes 49156
  0.7 120.2 %copy-start.1 = (s32[512,1]{0,1:T(1,128)S(1)}, s32[512,1]{0,1:T(1,128)}, u32[]{:S(2)}) copy-start(s32[512,1]{0,1:T(1,128)} %param.19) | copy-start | bytes 6148
  0.7 120.2 %copy-start.3 = (bf16[16,1,128,128]{3,2,1,0:T(8,128)(2,1)S(1)}, bf16[16,1,128,128]{3,2,1,0:T(8,128)(2,1)}, u32[]{:S(2)}) copy-start(bf16[16,1,128,128]{3,2,1,0:T(8,128)(2,1)} %param.18) | copy-start | bytes 1572868
  0.7 120.2 %copy-start.2 = (bf16[16,1,128,128]{3,2,1,0:T(8,128)(2,1)S(1)}, bf16[16,1,128,128]{3,2,1,0:T(8,128)(2,1)}, u32[]{:S(2)}) copy-start(bf16[16,1,128,128]{3,2,1,0:T(8,128)(2,1)} %param.17) | copy-start | bytes 1572868

commit v4 on v3

--- a/solution.py
+++ b/solution.py
@@ -127,7 +127,7 @@
 def exchange_kernel(
     rows,
     place,
-    ids,
+    ids_in,
     kept,
     counts,
     hid,
@@ -141,6 +141,7 @@
     nk_out,
     nv_out,
     flag,
+    ids,
     placed,
     table,
     tab,
@@ -353,6 +354,25 @@
 
     w_slot(1)
 
+    def whole_bf16(a):
+        return a.astype(jnp.float32).astype(jnp.bfloat16)
+
+    column = lax.broadcasted_iota(jnp.int32, (32, 64), 1)
+    for i in range(2):
+        chosen = whole_bf16(
+            (column == 2 * lax.broadcasted_iota(jnp.int32, (32, 64), 0) + i).astype(jnp.int32)
+        )
+        high, low = (
+            lax.dot_general(
+                chosen,
+                whole_bf16(digits),
+                (((1,), (1,)), ((), ())),
+                preferred_element_type=jnp.float32,
+            )
+            for digits in (ids_in[...] // 16, lax.rem(ids_in[...], 16))
+        )
+        ids[:, i * NDOC : (i + 1) * NDOC] = (high * 16.0 + low).astype(jnp.int32)
+
     def look_up(d, found):
         return jnp.where(ids[...] == d, place[d], found)
 
@@ -424,21 +444,23 @@
 
         lax.fori_loop(0, NZ, one, 0)
 
-    def send_docs_x(rank):
+    def send_docs_x(rank, kv=None):
         there = (xr1 if rank else xr).at[x]
         copies = []
         for k in range(1, NX):
-            i = rank * 3 + k - 1
-            copies.append(
-                go(send(xs.at[k - 1, rank], there, dx_s.at[i], dx_r.at[i], dev_x(k)))
-            )
+            here = xs.at[k - 1, rank]
+            i = rank * 6 + k - 1
+            if kv is not None:
+                i += kv * 3
+            src, dst = (here, there) if kv is None else (here.at[:, kv], there.at[:, kv])
+            copies.append(go(send(src, dst, dx_s.at[i], dx_r.at[i], dev_x(k))))
         return copies
 
     pack(1)
     docs_x1 = send_docs_x(1)
     w_slot(2)
     pack(0)
-    docs_x = send_docs_x(0)
+    docs_x = [send_docs_x(0, 0), send_docs_x(0, 1)]
     for copy in hx:
         copy.wait_recv()
     own_h.wait()
@@ -589,10 +611,10 @@
     w_slot(7)
     spare_step(3)
     spare_step(4)
-    for copy in docs_x:
-        copy.wait_recv()
     docs_z, own_z = ([], []), []
     for kv, held in ((0, zk), (1, zv)):
+        for copy in docs_x[kv]:
+            copy.wait_recv()
         for k in (4, 3, 5, 2, 6, 1, 7):
             i = kv * 7 + k - 1
             docs_z[kv].append(
@@ -685,7 +707,7 @@
         third(n)
         heads(n - 1)
     fetch(1, zv, values, nv_out)
-    lax.fori_loop(0, 8, gather_values, 0)
+    lax.fori_loop(0, 8, gather_values, 0, unroll=2)
     for copy in started:
         copy.wait_send()
 
@@ -709,6 +731,7 @@
         in_specs=[smem, smem, vmem, vmem, vmem, anym, anym, anym, anym, anym, anym],
         out_specs=(vmem, vmem, vmem, vmem, smem),
         scratch_shapes=[
+            pltpu.VMEM((32, 32), jnp.int32),
             pltpu.VMEM((32, 32), jnp.int32),
             pltpu.VMEM((32, 128), jnp.int32),
             pltpu.SMEM((32, 128), jnp.int32),
@@ -744,8 +767,8 @@
             dma((10,)),
             dma((10,)),
             dma((10,)),
-            dma((6,)),
-            dma((6,)),
+            dma((9,)),
+            dma((9,)),
             dma((14,)),
             dma((14,)),
             dma((10,)),
@@ -770,13 +793,10 @@
     doc_place,
     recompute_rows,
 ):
-    owners = lax.axis_size("req")
-    refs = 2 * NDOC
-    ids = doc_ids.reshape(owners, refs)
     attended, queries, keys_new, values_new, flag = fused(
         recompute_rows,
         doc_place,
-        ids,
+        doc_ids.T,
         kept_blocks.reshape(512, SLOTS).T,
         slot_counts.T,
         hidden.reshape(256, -1),

time: 127 us -> 124 us (0.976)
  local copies, waits for them, and re-layouts: 4.72 us -> 3.16 us
    unnamed x18 -> x17, local copies, waits for them, and re-layouts: 4.04 us -> 3.16 us
where the time goes in v4:
time: 124 us; the launch traced here: 122 us
  Pallas kernels  117 us (94%)
  local copies, waits for them, and re-layouts  3.16 us (3%)
  between operations  1.4 us (1%)
    pallas_call x1, Pallas kernels, fused(): pl.pallas_call(exchange_kernel, out_shape=(jax.ShapeDtypeStruct((256, 102...  117 us
    unnamed x17, local copies, waits for them, and re-layouts  3.16 us

profile of v4, /device:TPU:1, one launch (start us, length us, event | category | flops | bytes accessed | tf_op | source)
XLA Modules:
  0.0 122.2 jit_solution(1623675758175331344)
XLA Ops:
  0.6 0.0 copy-start.8
  0.6 0.0 copy-start
  0.7 0.0 copy-start.7
  0.7 0.0 copy-start.6
  0.7 0.0 copy-start.1
  0.7 0.0 copy-start.3
  0.7 0.0 copy-start.2
  0.7 117.4 %shard_map.130 = (bf16[256,1024]{1,0:T(8,128)(2,1)}, bf16[2048,128]{1,0:T(8,128)(2,1)}, bf16[256,128]{1,0:T(8,128)(2,1)S(1)}, bf16[256,128]{1,0:T(8,128)(2,1)S(1)}, s32[1,1]{1,0:T(1,128)}) custom-call(s32[2,128]{1,0:T(2,128)} %rows.1, s32[512]{0:T(512)} %place.1, s32[16,64]{1,0:T(8,128)} %bitcast.142, s32[8,512]{1,0:T(8,128)} %bitcast.141, ...), custom_call_target="tpu_custom_call" | custom-call | tf_op jit(solution)/shard_map/pallas_call | solution.py:722
  118.7 0.0 copy-done.8
  118.7 0.0 copy-done
  118.7 0.0 copy-done.7
  118.8 0.0 copy-done.6
  118.8 0.0 copy-done.1
  118.8 0.0 copy-done.3
  118.8 0.0 copy-done.2
  118.8 0.2 conditional.1
  119.0 1.9 %copy.73 = bf16[2,128,1024]{2,1,0:T(8,128)(2,1)} copy(bf16[2,128,1024]{2,1,0:T(8,128)(2,1)} %get-tuple-element.183) | data formatting | bytes 1048576
  120.9 0.6 copy.74
  121.5 0.6 copy.75
Async XLA Ops:
  0.6 118.1 %copy-start.8 = (s32[2,128]{1,0:T(2,128)S(1)}, s32[2,128]{1,0:T(2,128)}, u32[]{:S(2)}) copy-start(s32[2,128]{1,0:T(2,128)} %rows.1) | copy-start | bytes 3076
  0.6 118.1 %copy-start = (s32[512]{0:T(512)S(1)}, s32[512]{0:T(512)}, u32[]{:S(2)}) copy-start(s32[512]{0:T(512)} %place.1) | copy-start | bytes 6148
  0.7 118.1 %copy-start.7 = (s32[64,16]{0,1:T(8,128)S(1)}, s32[64,16]{0,1:T(8,128)}, u32[]{:S(2)}) copy-start(s32[64,16]{0,1:T(8,128)} %param.21) | copy-start | bytes 12292
  0.7 118.1 %copy-start.6 = (s32[512,1,8]{0,2,1:T(8,128)S(1)}, s32[512,1,8]{0,2,1:T(8,128)}, u32[]{:S(2)}) copy-start(s32[512,1,8]{0,2,1:T(8,128)} %param.20) | copy-start | bytes 49156
  0.7 118.1 %copy-start.1 = (s32[512,1]{0,1:T(1,128)S(1)}, s32[512,1]{0,1:T(1,128)}, u32[]{:S(2)}) copy-start(s32[512,1]{0,1:T(1,128)} %param.19) | copy-start | bytes 6148
  0.7 118.1 %copy-start.3 = (bf16[16,1,128,128]{3,2,1,0:T(8,128)(2,1)S(1)}, bf16[16,1,128,128]{3,2,1,0:T(8,128)(2,1)}, u32[]{:S(2)}) copy-start(bf16[16,1,128,128]{3,2,1,0:T(8,128)(2,1)} %param.18) | copy-start | bytes 1572868
  0.7 118.1 %copy-start.2 = (bf16[16,1,128,128]{3,2,1,0:T(8,128)(2,1)S(1)}, bf16[16,1,128,128]{3,2,1,0:T(8,128)(2,1)}, u32[]{:S(2)}) copy-start(bf16[16,1,128,128]{3,2,1,0:T(8,128)(2,1)} %param.17) | copy-start | bytes 1572868
